TPU v7x, 512 devices: a whole 4x4x16 slice. The times are simulated.
512 devices in a mesh: ctx: 32 (over y, x, core), tp: 16 (over z).
Axes of the slice: x: 4, y: 4, z: 16, core: 2. Of those that a mesh axis runs over, the one named last changes fastest.
Arguments:
- hidden: bfloat16 [2, 4096, 4096], P(None, 'ctx', 'tp'), may hold values from -6 to 6
- norm_gain: float32 [4096], replicated, may hold values from 0.5 to 1.5
- in_weight: bfloat16 [4096, 3, 4096], P('ctx', None, 'tp'), may hold values from -0.09375 to 0.09375
- short_weight: float32 [3, 3, 4096], P(None, None, 'tp'), may hold values from -4 to 4
- residues: float32 [16, 4096], P(None, 'tp'), may hold values from -5 to 5
- rates: float32 [16, 4096], P(None, 'tp'), may hold values from 7.324219e-05 to 0.05
- skip_gain: float32 [4096], P('tp'), may hold values from -4 to 4
- out_weight: bfloat16 [4096, 4096], P('tp', 'ctx'), may hold values from -0.09375 to 0.09375
- lengths: int32 [2], replicated, may hold values from 512 to 4096, as said below
Outputs:
- block_out: bfloat16 [2, 4096, 4096], P(None, 'ctx', 'tp')
Inputs may be any that keep to these rules, and one draw needn't show every extreme that they name: `lengths`: one of the 2 sequences, drawn from the seed, has all 4096 positions valid; the other has between 512 and 4096.
All inputs are finite; a program needn't handle non-finite values.
Results may differ from a plain program's by a relative error of at most 0.023.
Values may be sent and summed in bfloat16 or wider, within the bound.
A program may use at most 128 MiB of HBM per device.

v0:
```python
import math

import jax
import jax.numpy as jnp
import numpy as np
from jax import lax
from jax.sharding import PartitionSpec as P


def from_behind(value, axis, steps):
    count = lax.axis_size(axis)
    leading, last = (max(0, -steps), min(count, count - steps))
    return lax.ppermute(value, axis, [(source, source + steps) for source in range(leading, last)])


def on_device(
    hidden, norm_gain, in_weight, short_weight, residues, rates, skip_gain, out_weight, lengths
):
    samples, block, width = hidden.shape
    modes = rates.shape[0]
    taps = short_weight.shape[0]
    highest = lax.Precision.HIGHEST
    whole = lax.all_gather(hidden, "tp", axis=2, tiled=True)
    wf = whole.astype(jnp.float32)
    scale = lax.rsqrt(jnp.mean(wf * wf, axis=-1, keepdims=True) + 1e-06)
    normed = (wf * scale * norm_gain).astype(jnp.bfloat16)
    proj = jnp.einsum(
        "sbd,djc->sbjc",
        normed,
        lax.all_gather(in_weight, "ctx", axis=0, tiled=True),
        preferred_element_type=jnp.float32,
    ).astype(jnp.bfloat16)
    rim = from_behind(proj[:, block - (taps - 1) :], "ctx", 1)
    extended = jnp.concatenate([rim, proj], axis=1).astype(jnp.float32)
    feat = jnp.zeros((samples, block, 3, width), jnp.float32)
    for i in range(taps):
        feat = feat + short_weight[i] * extended[:, taps - 1 - i : taps - 1 - i + block]
    query, keys, values = (feat[:, :, 0], feat[:, :, 1], feat[:, :, 2])
    my_start = lax.axis_index("ctx") * block
    positions = my_start + jnp.arange(block, dtype=jnp.int32)
    valid = (positions[None, :] < lengths[:, None]).astype(jnp.float32)[..., None]
    inputs = (keys * values * valid).astype(jnp.bfloat16)
    in_float = inputs.astype(jnp.float32)
    coef = residues * jnp.sqrt(2.0 * rates / modes)
    sub = math.gcd(block, 16)
    groups = block // sub
    lag = jnp.arange(sub, dtype=jnp.float32)
    short_filter = jnp.einsum(
        "mc,nmc->nc", coef, jnp.exp(-rates[None] * lag[:, None, None]), precision=highest
    )
    differ = np.arange(sub)[:, None] - np.arange(sub)[None, :]
    toeplitz = jnp.where(
        jnp.asarray(differ >= 0)[:, :, None], short_filter[jnp.asarray(np.maximum(differ, 0))], 0.0
    )
    units = in_float.reshape(samples, groups, sub, width)
    intra = jnp.einsum("sgpc,tpc->sgtc", units, toeplitz, precision=highest)
    end_weight = jnp.exp(-rates[None] * (sub - 1.0 - lag)[:, None, None])
    group_sums = jnp.einsum("sgpc,pmc->gsmc", units, end_weight, precision=highest)
    step_decay = jnp.exp(-rates * sub)

    def advance(state, addend):
        return (step_decay[None] * state + addend, state)

    local_end, before = lax.scan(
        advance, jnp.zeros((samples, modes, width), jnp.float32), group_sums
    )
    span_weight = jnp.exp(
        -rates[None] * (block - 1.0 - jnp.arange(block, dtype=jnp.float32))[:, None, None]
    )
    piece = lax.all_gather(inputs, "ctx", axis=1, tiled=True)
    rows = piece.shape[1]
    count = -(-rows // block)
    padded_rows = count * block
    index = jnp.arange(padded_rows, dtype=jnp.int32)
    data = piece.astype(jnp.float32)
    data = jnp.where((index < my_start)[None, :, None], data, 0.0).reshape(
        samples, count, block, width
    )
    ends = jnp.einsum("sgjc,jmc->sgmc", data, span_weight, precision=highest)
    last = block * jnp.arange(count, dtype=jnp.int32) + block - 1
    distance = jnp.maximum(my_start - 1 - last, -block).astype(jnp.float32)
    factor = jnp.exp(-rates[None] * distance[:, None, None])
    incoming = jnp.einsum("sgmc,gmc->smc", ends, factor, precision=highest)
    group_decay = jnp.exp(
        -rates[None] * (sub * jnp.arange(groups, dtype=jnp.float32))[:, None, None]
    )
    state_in = before + group_decay[:, None] * incoming[None]
    carry_weight = coef[None] * jnp.exp(-rates[None] * (lag + 1.0)[:, None, None])
    cross = jnp.einsum("gsmc,tmc->sgtc", state_in, carry_weight, precision=highest)
    conv = (intra + cross).reshape(samples, block, width)
    gated = (query * (conv + skip_gain * in_float) * valid).astype(jnp.bfloat16)
    flat = gated.reshape(samples * block, width)
    piece = lax.all_gather(out_weight, "ctx", axis=1, tiled=True)
    partial_out = jnp.dot(flat, piece, preferred_element_type=jnp.float32).reshape(
        samples, block, piece.shape[1]
    )
    summed = lax.psum_scatter(
        partial_out.astype(jnp.bfloat16), "tp", scatter_dimension=2, tiled=True
    ).astype(jnp.float32)
    return (hidden.astype(jnp.float32) + summed).astype(jnp.bfloat16)


def solution(mesh):
    placed = (
        P(None, "ctx", "tp"),
        P(),
        P("ctx", None, "tp"),
        P(None, None, "tp"),
        P(None, "tp"),
        P(None, "tp"),
        P("tp"),
        P("tp", "ctx"),
        P(),
    )
    return jax.shard_map(
        on_device, mesh=mesh, in_specs=placed, out_specs=P(None, "ctx", "tp"), check_vma=False
    )
```

profile of v0, /device:TPU:6, one launch (start us, length us, event | category | flops | bytes accessed | tf_op | source)
XLA Modules:
  0.0 390.4 jit_solution(1303776743289339422)
XLA Ops:
  8.8 83.7 %all-gather.5.cloned.1.call-done = bf16[2,128,4096]{2,1,0:T(8,128)(2,1)} async-done(((bf16[2,128,256]{2,1,0:T(8,128)(2,1)}), bf16[2,128,4096]{2,1,0:T(8,128)(2,1)}) %all-gather.5.cloned.1.call-update) | async-done | bytes 2097168 | tf_op jit(solution)/shard_map/all_gather | solution.py:23
  92.5 2.2 fusion.2
  94.8 61.0 %all-gather.7.cloned.1.call-done = bf16[4096,3,256]{2,0,1:T(8,128)(2,1)} async-done(((bf16[128,3,256]{2,0,1:T(8,128)(2,1)}), bf16[4096,3,256]{2,0,1:T(8,128)(2,1)}) %all-gather.7.cloned.1.call-update) | async-done | bytes 6291472 | tf_op jit(solution)/shard_map/all_gather | solution.py:30
  155.8 4.6 %fusion.24 = bf16[2,128,3,256]{3,1,2,0:T(8,128)(2,1)S(1)} fusion(bf16[4096,3,256]{2,0,1:T(8,128)(2,1)} %all-gather.7.cloned.1.call-done, bf16[2,128,4096]{2,1,0:T(8,128)(2,1)S(1)} %copy-done.2, f32[4096]{0:T(1024)S(1)} %copy-done.11, f32[2,128]{1,0:T(2,128)S(1)} %add_rsqrt_fusion), kind=kOutput, calls=%fused_computation.33 | convolution fusion | flops 1615003648 | bytes 8799232 | tf_op jit(solution)/shard_map/sbd,djc->sbjc/dot_general | solution.py:27
  160.4 2.1 collective-permute-start
  162.7 2.7 collective-permute-done
  168.7 2.3 copy.36
  174.3 2.4 copy.21
  176.7 1.3 copy.22
  178.0 2.8 fusion.7
  180.8 2.5 copy.35
  183.3 5.2 %while.13 = (s32[]{:T(128)}, f32[2,16,256]{2,1,0:T(8,128)S(1)}, f32[8,2,16,256]{3,2,1,0:T(8,128)}, f32[16,256]{1,0:T(8,128)S(1)}, f32[8,2,16,256]{3,2,1,0:T(8,128)S(1)}, /*index=5*/s32[]{:T(128)}, s32[]{:T(128)}) while((s32[]{:T(128)}, f32[2,16,256]{2,1,0:T(8,128)S(1)}, f32[8,2,16,256]{3,2,1,0:T(8,128)}, f32[16,256]{1,0:T(8,128)S(1)}, ...), condition=%wide.region_2.3_spmd.clone, body=%wide.region_1.2_spmd.clone.sunk | while | flops 32771 | bytes 180828 | solution.py:64
  188.5 40.9 %all-gather.9.cloned.1.call-done = bf16[2,4096,256]{2,1,0:T(8,128)(2,1)} async-done(((bf16[2,128,256]{2,1,0:T(8,128)(2,1)}), bf16[2,4096,256]{2,1,0:T(8,128)(2,1)}) %all-gather.9.cloned.1.call-update) | async-done | bytes 4194320 | tf_op jit(solution)/shard_map/all_gather | solution.py:70
  229.4 5.3 %convert_select_fusion = f32[2,4096,256]{2,1,0:T(8,128)} fusion(bf16[2,4096,256]{2,1,0:T(8,128)(2,1)} %all-gather.9.cloned.1.call-done, pred[4096]{0:T(1024)(128)(4,1)S(1)} %iota_compare_fusion), kind=kLoop, calls=%fused_computation.3 | loop fusion | flops 4194304 | bytes 12587008 | tf_op jit(solution)/shard_map/jit(_where)/select_n | solution.py:76
  234.7 10.7 %copy.37 = f32[2,32,128,256]{2,1,0,3:T(8,128)} copy(f32[2,32,128,256]{3,2,1,0:T(8,128)} %bitcast.93) | data formatting | bytes 16777216 | tf_op jit(solution)/shard_map/reshape | solution.py:76
  245.5 38.7 %convolution_bitcast_fusion = f32[16,256,32,2]{2,0,3,1:T(8,128)} fusion(f32[128,16,256,1]{0,1,3,2:T(8,128)} %copy.36, f32[2,32,128,256]{2,1,0,3:T(8,128)} %copy.37), kind=kOutput, calls=%fused_computation.12 | convolution fusion | flops 402653184 | bytes 11534336 | tf_op jit(solution)/shard_map/sgjc,jmc->sgmc/dot_general | solution.py:79
  284.2 3.7 copy.43
  290.1 2.5 copy.24
  292.6 5.5 %fusion.9 = f32[256,16,8,2]{1,2,3,0:T(8,128)S(1)} fusion(f32[8,2,16,256]{2,0,1,3:T(8,128)} %copy.24, f32[16]{0:T(128)S(1)} %iota_add_fusion.1, f32[16,256]{0,1:T(8,128)S(1)} %copy.23, f32[16,256]{0,1:T(8,128)S(1)} %copy.20), kind=kOutput, calls=%fused_computation.16 | convolution fusion | flops 12713984 | bytes 557120 | tf_op jit(solution)/shard_map/gsmc,tmc->sgtc/dot_general | solution.py:89
  298.2 3.3 bitcast_add_fusion.1
  301.4 2.5 copy.25
  305.1 3.6 convolution_convert_fusion
  308.7 73.3 %reduce-scatter.2.cloned.1.call-done = bf16[2,128,256]{2,1,0:T(8,128)(2,1)} async-done(((bf16[2,128,4096]{2,1,0:T(8,128)(2,1)}), bf16[2,128,256]{2,1,0:T(8,128)(2,1)}) %reduce-scatter.2.cloned.1.call-update) | async-done | bytes 131088 | tf_op jit(solution)/shard_map/reduce_scatter | solution.py:97
  382.0 1.6 add_convert_fusion
  (85 shorter events, 17.1 us)
Async XLA Ops:
  6.5 149.3 %copy-start.11 = (f32[4096]{0:T(1024)S(1)}, f32[4096]{0:T(1024)}, u32[]{:S(2)}) copy-start(f32[4096]{0:T(1024)} %param.14) | copy-start | bytes 49156
  6.5 86.0 %all-gather.5.cloned.1.call-start = ((), (), s32[]{:S(2)}) async-start(), calls=%async_computation.1 | async-start | bytes 2228224 | tf_op jit(solution)/shard_map/all_gather | solution.py:23
  7.3 148.5 %all-gather.7.cloned.1.call-start = ((), (), s32[]{:S(2)}) async-start(), calls=%async_computation.2 | async-start | bytes 6488064 | tf_op jit(solution)/shard_map/all_gather | solution.py:30
  8.0 221.4 %all-gather.9.cloned.1.call-start = ((), (), s32[]{:S(2)}) async-start(), calls=%async_computation.3 | async-start | bytes 4325376 | tf_op jit(solution)/shard_map/all_gather | solution.py:70
  92.5 63.3 %copy-start.2 = (bf16[2,128,4096]{2,1,0:T(8,128)(2,1)S(1)}, bf16[2,128,4096]{2,1,0:T(8,128)(2,1)}, u32[]{:S(2)}) copy-start(bf16[2,128,4096]{2,1,0:T(8,128)(2,1)} %all-gather.5.cloned.1.call-done) | copy-start | bytes 6291460
  94.8 67.8 %copy-start.7 = (s32[2]{0:T(128)S(1)}, s32[2]{0:T(128)}, u32[]{:S(2)}) copy-start(s32[2]{0:T(128)} %param.21) | copy-start | bytes 28
  160.4 4.9 %collective-permute-start = (bf16[2,2,3,256]{3,1,2,0:T(2,128)(2,1)S(1)}, bf16[2,2,3,256]{3,1,2,0:T(2,128)(2,1)S(1)}, u32[]{:S(2)}, u32[]{:S(2)}) collective-permute-start(bf16[2,2,3,256]{3,1,2,0:T(2,128)(2,1)S(1)} %slice.42), channel_id=1, source_target_pairs={{0,16},{16,32},{32,48},{48,64},{64,80},{80,96},{96,112},{112,128},... | collective-permute-start | bytes 18440 | tf_op jit(solution)/shard_map/ppermute | solution.py:13
  165.5 2.7 copy-start.5
  165.5 2.7 copy-start.6
  165.8 0.9 copy-start.1
  167.4 137.6 %all-gather.11.cloned.1.call-start = ((), (), s32[]{:S(2)}) async-start(), calls=%async_computation.4 | async-start | bytes 2162688 | tf_op jit(solution)/shard_map/all_gather | solution.py:93
  168.0 214.0 %reduce-scatter.2.cloned.1.call-start = ((), (), s32[]{:S(2)}) async-start(), calls=%async_computation.5 | async-start | bytes 2228224 | tf_op jit(solution)/shard_map/reduce_scatter | solution.py:97
  171.0 2.3 copy-start.10
  292.6 5.6 %copy-start = (f32[16,16,256]{1,0,2:T(8,128)S(1)}, f32[16,16,256]{1,0,2:T(8,128)}, u32[]{:S(2)}) copy-start(f32[16,16,256]{1,0,2:T(8,128)} %copy.21) | copy-start | bytes 786436
  292.6 5.6 %copy-start.8 = (pred[16,16]{1,0:T(8,128)(4,1)S(1)}, pred[16,16]{1,0:T(8,128)(4,1)}, u32[]{:S(2)}) copy-start(pred[16,16]{1,0:T(8,128)(4,1)} %constant.59.clone) | copy-start | bytes 772
  301.4 2.5 copy-start.3
  301.4 2.5 copy-start.9
  308.7 73.3 %copy-start.4 = (bf16[2,128,256]{2,1,0:T(8,128)(2,1)S(1)}, bf16[2,128,256]{2,1,0:T(8,128)(2,1)}, u32[]{:S(2)}) copy-start(bf16[2,128,256]{2,1,0:T(8,128)(2,1)} %param.13) | copy-start | bytes 393220
Sparse Core Ops, SparseCore 0:
  9.4 83.1 all-gather.4
  95.7 60.0 all-gather.6
  167.6 61.7 all-gather.8
  232.3 59.5 all-gather.10
  308.8 73.1 reduce-scatter.1
where the time goes:
time: 398 us; the launch traced here: 390 us
  waiting for transfers between devices  264 us (66%)
  matrix products  58.6 us (15%)
  local copies, waits for them, and re-layouts  32 us (8%)
  other arithmetic  20 us (5%)
  between operations  13.7 us (3%)
    all_gather x1, waiting for transfers between devices, on_device(): whole = lax.all_gather(hidden, 'tp', axis=2, tiled=True)  83.7 us
    reduce_scatter x1, waiting for transfers between devices, on_device(): lax.psum_scatter(partial_out.astype(jnp.bfloat16), 'tp', scatter_dimensio...  73.3 us
    all_gather x1, waiting for transfers between devices, on_device(): lax.all_gather(in_weight, 'ctx', axis=0, tiled=True)  61 us
    all_gather x1, waiting for transfers between devices, on_device(): piece = lax.all_gather(inputs, 'ctx', axis=1, tiled=True)  40.9 us
    dot_general x1, matrix products, on_device(): ends = jnp.einsum('sgjc,jmc->sgmc', data, span_weight, precision=highest)  38.7 us
    reshape x1, local copies, waits for them, and re-layouts, on_device(): jnp.where((index < my_start)[None, :, None], data, 0.0)  10.7 us
  transfers between devices with their start and end apart: 6, of which 5 were waited for; matrix products, arithmetic and copies ran while one was open for 25% of the time, Pallas kernels for 0%

commit v1 on v0

v1 whole, which is shorter than its diff:
```python
import functools

import jax
import jax.numpy as jnp
from jax import lax
from jax.experimental import pallas as pl
from jax.experimental.pallas import tpu as pltpu
from jax.sharding import PartitionSpec as P

MESH = pl.DeviceIdType.MESH
F32, BF16 = jnp.float32, jnp.bfloat16
RIGHT, LEFT = 0, 1


def rem(a, b):
    return lax.rem(a, jnp.int32(b))


def div(a, b):
    return lax.div(a, jnp.int32(b))


def remote(src, dst, send_sem, recv_sem, device):
    return pltpu.make_async_remote_copy(
        src_ref=src, dst_ref=dst, send_sem=send_sem, recv_sem=recv_sem,
        device_id=device, device_id_type=MESH,
    )


def kernel(
    side, hid_hbm, w_hbm, ow_hbm, gain_ref, taps_ref, res_ref, rates_ref, skip_ref, len_ref, out_ref,
    hraw, hs, pbuf, ssq, acc, ext, qbuf, ubuf, cbuf, gated, st0, st1, st2, rs_out, rs_in,
    load_sem, ag_send, ag_recv, sib_send, sib_recv, rim_send, rim_recv,
    st0_send, st0_recv, st1_send, st1_recv, st2_send, st2_recv, rs_send, rs_recv,
):
    n = side * side
    half = n // 2
    samples, block, width = hid_hbm.shape
    rows = pbuf.shape[1]
    modes = rates_ref.shape[0]
    features = n * width
    me = lax.axis_index("ctx")
    z = lax.axis_index("tp")
    core = rem(me, 2)
    chip = div(me, 2)
    y, x = div(chip, side), rem(chip, side)
    turn = rem(x + y, side)
    sibling = {"ctx": me + 1 - 2 * core}

    def at(yy, xx):
        return {"ctx": 2 * (side * yy + xx) + core}

    def chip_first(q):
        a = div(q, side)
        return side * a + rem(q - side * a + side - a, side)

    def chip_second(q):
        a = div(q, side)
        return side * rem(q - side * a + side - a, side) + a

    def from_last(steps):
        return rem(me + 2 * n - steps, 2 * n)

    quarter = rows // 4
    rings = [
        (z, lambda q: {"tp": q}, lambda q, c: hraw.at[q, c]),
        (
            side * y + turn,
            lambda q: {"ctx": 2 * chip_first(q) + core},
            lambda q, c: pbuf.at[2 * chip_first(q) + core, pl.ds(quarter * c, quarter)],
        ),
        (
            side * x + turn,
            lambda q: {"ctx": 2 * chip_second(q) + core},
            lambda q, c: pbuf.at[2 * chip_second(q) + core, pl.ds(2 * quarter + quarter * c, quarter)],
        ),
    ]
    cycle_chip = [None, chip_first, chip_second]

    def owner(r, way, s):
        place = rings[r][0]
        return rem(place + n - s, n) if way == RIGHT else rem(place + s, n)

    def ag_start(r, way, s, c):
        place, device, view = rings[r]
        to = rem(place + 1, n) if way == RIGHT else rem(place + n - 1, n)
        block_ref = view(owner(r, way, s - 1), c)
        remote(block_ref, block_ref, ag_send.at[r, way, s - 1, c], ag_recv.at[r, way, s - 1, c], device(to)).start()

    def ag_arrived(r, way, s, c):
        place, device, view = rings[r]
        block_ref = view(owner(r, way, s), c)
        remote(block_ref, block_ref, ag_send.at[r, way, s - 1, c], ag_recv.at[r, way, s - 1, c], device(place)).wait_recv()

    def sib_view(r, way, s, which):
        return pbuf.at[
            2 * cycle_chip[r](owner(r, way, s)) + which, pl.ds(2 * quarter * (r - 1), 2 * quarter)
        ]

    def sib_start(r, way, s):
        part = sib_view(r, way, s, core)
        remote(part, part, sib_send.at[r - 1, way, s], sib_recv.at[r - 1, way, s], sibling).start()

    def sib_wait(r, way, s):
        part = sib_view(r, way, s, 1 - core)
        copy = remote(part, part, sib_send.at[r - 1, way, s], sib_recv.at[r - 1, way, s], sibling)
        copy.wait_send()
        copy.wait_recv()

    loads = [pltpu.make_async_copy(hid_hbm, hraw.at[z], load_sem.at[0])]
    for j in range(3):
        loads.append(pltpu.make_async_copy(
            w_hbm.at[j], pbuf.at[me, :, pl.ds(width * j, width)], load_sem.at[1 + j]))
    for j in range(2):
        loads.append(pltpu.make_async_copy(
            ow_hbm.at[pl.ds(rows * j, rows)], pbuf.at[me, :, pl.ds(3 * width + rows * j, rows)], load_sem.at[4 + j]))
    for copy in loads:
        copy.start()
    partners = [{"tp": rem(z + 1, n)}, {"tp": rem(z + n - 1, n)}, sibling, {"ctx": from_last(1)}]
    for j in range(1, side):
        partners.append(at(y, rem(x + j, side)))
        partners.append(at(rem(y + j, side), x))
    barrier = pltpu.get_barrier_semaphore()
    for partner in partners:
        pl.semaphore_signal(barrier, inc=1, device_id=partner, device_id_type=MESH)
    for copy in loads:
        copy.wait()
    pl.semaphore_wait(barrier, len(partners))

    def take(q):
        gain = gain_ref[pl.ds(q, 1), :]
        for s in range(samples):
            value = hraw[q, s].astype(F32)
            span = pl.ds(s * block, block)
            square = value * value
            ssq[span, :] = ssq[span, :] + square[:, : width // 2] + square[:, width // 2 :]
            hs[span, pl.ds(pl.multiple_of(q * width, width), width)] = (value * gain).astype(BF16)

    chunks = [(r, way, c) for c in range(2) for r in range(3) for way in (RIGHT, LEFT)]
    for r, way, c in chunks:
        ag_start(r, way, 1, c)
    for r in (1, 2):
        sib_start(r, RIGHT, 0)
    ssq[...] = jnp.zeros_like(ssq)
    take(z)

    def ag_step(s, carry):
        for r, way, c in chunks:
            ag_arrived(r, way, s, c)
            ag_start(r, way, s + 1, c)
        for r in (1, 2):
            for way in (RIGHT, LEFT):
                sib_start(r, way, s)
        take(owner(0, RIGHT, s))
        take(owner(0, LEFT, s))
        return carry

    lax.fori_loop(1, half - 1, ag_step, 0)
    for r, way, c in chunks:
        ag_arrived(r, way, half - 1, c)
        if c == way:
            ag_start(r, way, half, c)
    for r in (1, 2):
        for way in (RIGHT, LEFT):
            sib_start(r, way, half - 1)
    take(owner(0, RIGHT, half - 1))
    take(owner(0, LEFT, half - 1))
    for r in (1, 2, 0):
        for way in (RIGHT, LEFT):
            ag_arrived(r, way, half, way)
        if r:
            sib_start(r, RIGHT, half)
    take(owner(0, RIGHT, half))
    for r in (1, 2):
        sib_wait(r, RIGHT, 0)
        sib_wait(r, RIGHT, half)

    def sib_step(s, carry):
        for r in (1, 2):
            for way in (RIGHT, LEFT):
                sib_wait(r, way, s)
        return carry

    lax.fori_loop(1, half, sib_step, 0)

    deep = 4 if n % 4 == 0 else 1
    span_k = deep * width

    def product(i):
        left = hs[:, pl.ds(pl.multiple_of(i * span_k, span_k), span_k)]
        per = span_k // rows
        right = pbuf[pl.ds(i * per, per), :, : 3 * width].reshape(span_k, 3 * width)
        return jnp.dot(left, right, preferred_element_type=F32)

    acc[...] = product(jnp.int32(0))

    def project(i, carry):
        acc[...] = acc[...] + product(i)
        return carry

    lax.fori_loop(1, n // deep, project, 0)
    mean = jnp.sum(ssq[...], axis=1, keepdims=True) * (1.0 / features)
    scale = lax.rsqrt(mean + 1e-6)
    for s in range(samples):
        ext[s, 8:, :] = acc[s * block : (s + 1) * block, :] * scale[s * block : (s + 1) * block, :]
    rim = remote(ext.at[:, pl.ds(block, 8)], ext.at[:, pl.ds(0, 8)], rim_send, rim_recv, {"ctx": rem(me + 1, 2 * n)})
    rim.start()

    rates = rates_ref[...]
    decay = jnp.exp(-rates)
    whole = jnp.exp(-rates * float(block))
    coef = res_ref[...] * jnp.sqrt(2.0 * rates / modes)

    def powers(place, blocks):
        before, total = [], []
        for i in range(side):
            gap = jnp.maximum(place - 1 - i, 0).astype(F32)
            factor = jnp.exp(-rates * (gap * float(blocks * block)))
            before.append(jnp.where(i < place, factor, 0.0))
            total.append(jnp.exp(-rates * float(blocks * block * (side - 1 - i))))
        return before, total

    x_before, x_total = powers(x, 2)
    y_before, _ = powers(y, 2 * side)
    x_power = jnp.exp(-rates * (x.astype(F32) * float(2 * block)))

    rim.wait_recv()
    for s in range(samples):
        ext[s, :8, :] = jnp.where(me == 0, 0.0, ext[s, :8, :])

    def filtered(s, j):
        total = None
        for i in range(3):
            term = taps_ref[3 * i + j : 3 * i + j + 1, :] * ext[s, 8 - i : 8 - i + block, j * width : (j + 1) * width]
            total = term if total is None else total + term
        return total

    for s in range(samples):
        place = lax.broadcasted_iota(jnp.int32, (block, 1), 0) + me * block
        valid = jnp.where(place < len_ref[s], 1.0, 0.0)
        ubuf[s] = (filtered(s, 1) * filtered(s, 2) * valid).astype(BF16).astype(F32)
        qbuf[s] = filtered(s, 0) * valid

    def gather_state(g, states):
        states = list(states)
        tiles = [ubuf[s, pl.ds(pl.multiple_of(8 * g, 8), 8), :] for s in range(samples)]
        for i in range(8):
            for s in range(samples):
                states[s] = decay * states[s] + tiles[s][i : i + 1, :]
        return tuple(states)

    zero = jnp.zeros((modes, width), F32)
    ends = lax.fori_loop(0, block // 8, gather_state, (zero,) * samples)
    for s in range(samples):
        st0[core, s] = ends[s]
    pair = remote(st0.at[core], st0.at[core], st0_send, st0_recv, sibling)
    pair.start()
    pair_in = remote(st0.at[1 - core], st0.at[1 - core], st0_send, st0_recv, sibling)
    pair_in.wait_recv()
    for s in range(samples):
        st1[x, s] = whole * st0[0, s] + st0[1, s]
    for j in range(1, side):
        remote(st1.at[x], st1.at[x], st1_send.at[j], st1_recv.at[j], at(y, rem(x + j, side))).start()
    for j in range(1, side):
        slot = st1.at[rem(x + side - j, side)]
        remote(slot, slot, st1_send.at[j], st1_recv.at[j], sibling).wait_recv()
    for s in range(samples):
        st2[y, s] = sum(x_total[i] * st1[i, s] for i in range(side))
    for j in range(1, side):
        remote(st2.at[y], st2.at[y], st2_send.at[j], st2_recv.at[j], at(rem(y + j, side), x)).start()
    for j in range(1, side):
        slot = st2.at[rem(y + side - j, side)]
        remote(slot, slot, st2_send.at[j], st2_recv.at[j], sibling).wait_recv()
    incoming = []
    for s in range(samples):
        row = sum(y_before[i] * st2[i, s] for i in range(side))
        at_chip = x_power * row + sum(x_before[i] * st1[i, s] for i in range(side))
        incoming.append(jnp.where(core == 0, at_chip, whole * at_chip + st0[0, s]))

    def convolve(g, states):
        states = list(states)
        span = pl.ds(pl.multiple_of(8 * g, 8), 8)
        for s in range(samples):
            tile = ubuf[s, span, :]
            lines = []
            for i in range(8):
                states[s] = decay * states[s] + tile[i : i + 1, :]
                lines.append(jnp.sum(coef * states[s], axis=0, keepdims=True))
            cbuf[s, span, :] = jnp.concatenate(lines, axis=0)
        return tuple(states)

    lax.fori_loop(0, block // 8, convolve, tuple(incoming))
    for s in range(samples):
        gated[s] = (qbuf[s] * (cbuf[s] + skip_ref[...] * ubuf[s])).astype(BF16)

    def share(d, c):
        first, second = pbuf[2 * d, :, 3 * width :], pbuf[2 * d + 1, :, 3 * width :]
        right = jnp.concatenate([
            jnp.concatenate([first[:, :rows], second[:, :rows]], axis=1),
            jnp.concatenate([first[:, rows:], second[:, rows:]], axis=1),
        ], axis=0)
        return jnp.dot(gated[c], right, preferred_element_type=F32)

    def rs_copy(way, s, c):
        to = rem(z + 1, n) if way == RIGHT else rem(z + n - 1, n)
        return remote(
            rs_out.at[way, s - 1, c], rs_in.at[way, s - 1, c],
            rs_send.at[way, s - 1, c], rs_recv.at[way, s - 1, c], {"tp": to},
        )

    def rs_step(s, way, c, first):
        ahead = half + 1 - s
        d = rem(z + ahead, n) if way == RIGHT else rem(z + n - ahead, n)
        part = share(d, c)
        if not first:
            rs_copy(way, s - 1, c).wait_recv()
            part = part + rs_in[way, s - 2, c].astype(F32)
        rs_out[way, s - 1, c] = part.astype(BF16)
        rs_copy(way, s, c).start()

    for c in range(2):
        rs_step(1, c, c, True)
    for way, c in ((RIGHT, 1), (LEFT, 0), (RIGHT, 0), (LEFT, 1)):
        rs_step(2, way, c, way != c)

    def reduce_step(s, carry):
        for way, c in ((RIGHT, 1), (LEFT, 0), (RIGHT, 0), (LEFT, 1)):
            rs_step(s, way, c, False)
        return carry

    lax.fori_loop(3, half + 1, reduce_step, 0)
    for c in range(samples):
        part = share(z, c) + hraw[z, c].astype(F32)
        for way in (RIGHT, LEFT):
            rs_copy(way, half, c).wait_recv()
            part = part + rs_in[way, half - 1, c].astype(F32)
        out_ref[c] = part.astype(BF16)

    def ag_sent(r, way, s, c):
        place, device, view = rings[r]
        block_ref = view(owner(r, way, s - 1), c)
        remote(block_ref, block_ref, ag_send.at[r, way, s - 1, c], ag_recv.at[r, way, s - 1, c], device(place)).wait_send()

    def sent(s, carry):
        for r, way, c in chunks:
            ag_sent(r, way, s, c)
        return carry

    lax.fori_loop(1, half, sent, 0)
    for r in range(3):
        for way in (RIGHT, LEFT):
            ag_sent(r, way, half, way)
    rim.wait_send()
    pair.wait_send()
    for j in range(1, side):
        remote(st1.at[x], st1.at[x], st1_send.at[j], st1_recv.at[j], sibling).wait_send()
        remote(st2.at[y], st2.at[y], st2_send.at[j], st2_recv.at[j], sibling).wait_send()
    for c in range(2):
        rs_copy(c, 1, c).wait_send()

    def reduced(s, carry):
        for way in (RIGHT, LEFT):
            for c in range(2):
                rs_copy(way, s, c).wait_send()
        return carry

    lax.fori_loop(2, half + 1, reduced, 0)


def on_device(hidden, norm_gain, in_weight, short_weight, residues, rates, skip_gain, out_weight, lengths):
    samples, block, width = hidden.shape
    rows = in_weight.shape[0]
    n = lax.axis_size("tp")
    side = int(round(n ** 0.5))
    half = n // 2
    modes = rates.shape[0]
    dma = pltpu.SemaphoreType.DMA
    hbm = pl.BlockSpec(memory_space=pl.ANY)
    vmem = pl.BlockSpec(memory_space=pltpu.VMEM)
    state = (samples, modes, width)
    return pl.pallas_call(
        functools.partial(kernel, side),
        out_shape=jax.ShapeDtypeStruct(hidden.shape, BF16),
        in_specs=[hbm, hbm, hbm] + [vmem] * 5 + [pl.BlockSpec(memory_space=pltpu.SMEM)],
        out_specs=vmem,
        scratch_shapes=[
            pltpu.VMEM((n, samples, block, width), BF16),
            pltpu.VMEM((samples * block, n * width), BF16),
            pltpu.VMEM((2 * n, rows, 3 * width + 2 * rows), BF16),
            pltpu.VMEM((samples * block, width // 2), F32),
            pltpu.VMEM((samples * block, 3 * width), F32),
            pltpu.VMEM((samples, block + 8, 3 * width), F32),
            pltpu.VMEM((samples, block, width), F32),
            pltpu.VMEM((samples, block, width), F32),
            pltpu.VMEM((samples, block, width), F32),
            pltpu.VMEM((samples, block, width), BF16),
            pltpu.VMEM((2,) + state, F32),
            pltpu.VMEM((side,) + state, F32),
            pltpu.VMEM((side,) + state, F32),
            pltpu.VMEM((2, half, 2, block, width), BF16),
            pltpu.VMEM((2, half, 2, block, width), BF16),
            dma((6,)),
            dma((3, 2, half, 2)),
            dma((3, 2, half, 2)),
            dma((2, 2, half + 1)),
            dma((2, 2, half + 1)),
            dma,
            dma,
            dma,
            dma,
            dma((side,)),
            dma((side,)),
            dma((side,)),
            dma((side,)),
            dma((2, half, 2)),
            dma((2, half, 2)),
        ],
        compiler_params=pltpu.CompilerParams(
            collective_id=0, has_side_effects=True, vmem_limit_bytes=48 * 2**20
        ),
    )(
        hidden,
        jnp.transpose(in_weight, (1, 0, 2)),
        out_weight,
        norm_gain.reshape(n, width),
        short_weight.reshape(-1, width),
        residues,
        rates,
        skip_gain.reshape(1, width),
        lengths,
    )


def solution(mesh):
    placed = (
        P(None, "ctx", "tp"),
        P(),
        P("ctx", None, "tp"),
        P(None, None, "tp"),
        P(None, "tp"),
        P(None, "tp"),
        P("tp"),
        P("tp", "ctx"),
        P(),
    )
    return jax.shard_map(
        on_device, mesh=mesh, in_specs=placed, out_specs=P(None, "ctx", "tp"), check_vma=False
    )
```

time: 398 us -> 105 us (0.26); the launches traced: 390 us -> 103 us
  waiting for transfers between devices: 264 us -> 0 us
  Pallas kernels: 0 us -> 98.7 us
  matrix products: 58.6 us -> 0 us
  local copies, waits for them, and re-layouts: 32 us -> 4.76 us
  other arithmetic: 20 us -> 0 us
  between operations: 13.7 us -> 0.05 us
    all_gather x4 -> x0, waiting for transfers between devices: 186 us -> none  [the longest x1 83.7 us: on_device(): whole = lax.all_gather(hidden, 'tp', axis=2, tiled=True)]
    pallas_call x0 -> x1, Pallas kernels: none -> 98.7 us  [on_device(): pl.pallas_call(functools.partial(kernel, side), out_shape=jax.ShapeDtypeS...]
    reduce_scatter x1 -> x0, waiting for transfers between devices: 73.3 us -> none  [on_device(): lax.psum_scatter(partial_out.astype(jnp.bfloat16), 'tp', scatter_dimensio...]
    dot_general x6 -> x0, matrix products: 58.6 us -> none  [the longest x1 38.7 us: on_device(): ends = jnp.einsum('sgjc,jmc->sgmc', data, span_weight, precision=highest)]
    reshape x1 -> x2, local copies, waits for them, and re-layouts: 10.7 us -> 0.75 us  [the longest x1 0.74 us: on_device(): norm_gain.reshape(n, width)]
    select_n x1 -> x0, other arithmetic: 5.3 us -> none  [on_device(): jnp.where((index < my_start)[None, :, None], data, 0.0)]
    add x2 -> x0, local copies, waits for them, and re-layouts: 4.99 us -> none  [the longest x1 2.52 us: on_device(): conv = (intra + cross).reshape(samples, block, width)]
    dynamic_update_slice x8 -> x0, other arithmetic: 4.98 us -> none  [on_device(): lax.scan(advance, jnp.zeros((samples, modes, width), jnp.float32), group_...]
  transfers between devices with their start and end apart: 6 -> 0, of which waited for: 5 -> 0; matrix products, arithmetic and copies ran while one was open for 25% -> 0% of each run, Pallas kernels for 0% -> 0%
where the time goes in v1:
time: 105 us; the launch traced here: 103 us
  Pallas kernels  98.7 us (94%)
  local copies, waits for them, and re-layouts  4.76 us (5%)
    pallas_call x1, Pallas kernels, on_device(): pl.pallas_call(functools.partial(kernel, side), out_shape=jax.ShapeDtypeS...  98.7 us
    unnamed x17, local copies, waits for them, and re-layouts  4.01 us

profile of v1, /device:TPU:6, one launch (start us, length us, event | category | flops | bytes accessed | tf_op | source)
XLA Modules:
  0.0 103.5 jit_solution(5483611906760055106)
XLA Ops:
  0.0 0.0 copy-start.7
  0.0 0.0 copy-start.4
  0.0 0.7 reshape.9.gain_ref
  0.7 0.0 copy-done.7
  0.8 0.0 copy-start.3
  0.8 0.0 copy-start.5
  0.8 0.0 copy-start.6
  0.8 0.0 copy-done.4
  0.8 0.7 copy-done.3
  1.5 0.0 copy-done.5
  1.5 0.0 copy-done.6
  1.5 0.0 copy-start
  1.5 0.9 copy-done
  2.4 0.0 copy-start.1
  2.4 0.9 copy-done.1
  3.3 0.0 copy-start.2
  3.3 0.8 copy-done.2
  4.1 98.7 %shard_map.91 = bf16[2,128,256]{2,1,0:T(8,128)(2,1)S(1)} custom-call(bf16[2,128,256]{2,1,0:T(8,128)(2,1)S(1)} %copy-done.1, bf16[3,128,256]{2,1,0:T(8,128)(2,1)S(1)} %bitcast.2, bf16[256,128]{1,0:T(8,128)(2,1)S(1)} %copy-done.2, f32[16,256]{1,0:T(8,128)S(1)} %reshape.9.gain_ref, f32[9,256]{1,0:T(8,128)S(1)} %reshape.10.taps_ref, f32[16,256]{1,0:T(8,128)S(1)} %copy-done.3, ...), custom_call_target="tpu_custom_call" | custom-call | tf_op jit(solution)/shard_map/pallas_call | solution.py:381
  102.8 0.7 copy.11
  (1 shorter events, 0.0 us)
Async XLA Ops:
  0.0 0.7 copy-start.7
  0.0 0.8 copy-start.4
  0.8 0.7 copy-start.3
  0.8 0.7 copy-start.5
  0.8 0.7 copy-start.6
  1.5 0.9 copy-start
  2.4 0.9 copy-start.1
  3.3 0.8 copy-start.2

commit v2 on v1

v2 whole, which is shorter than its diff:
```python
import functools

import jax
import jax.numpy as jnp
from jax import lax
from jax.experimental import pallas as pl
from jax.experimental.pallas import tpu as pltpu
from jax.sharding import PartitionSpec as P

MESH = pl.DeviceIdType.MESH
F32, BF16 = jnp.float32, jnp.bfloat16
RIGHT, LEFT = 0, 1
CHUNKS = 4


def rem(a, b):
    return lax.rem(a, jnp.int32(b))


def div(a, b):
    return lax.div(a, jnp.int32(b))


def remote(src, dst, send_sem, recv_sem, device):
    return pltpu.make_async_remote_copy(
        src_ref=src, dst_ref=dst, send_sem=send_sem, recv_sem=recv_sem,
        device_id=device, device_id_type=MESH,
    )


def kernel(
    side, hid_hbm, w_hbm, ow_hbm, gain_hbm, taps_hbm, res_hbm, rates_hbm, skip_hbm, len_ref, out_ref,
    gain_ref, taps_ref, res_ref, rates_ref, skip_ref,
    hraw, hs, pbuf, ssq, acc, ext, qbuf, ubuf, cbuf, gated, table, st_in, st0, st1, st2, parts, rs_out, rs_in,
    load_sem, ag_send, ag_recv, sib_send, sib_recv, rim_send, rim_recv,
    st0_send, st0_recv, st1_send, st1_recv, st2_send, st2_recv, rs_send, rs_recv,
):
    n = side * side
    half = n // 2
    samples, block, width = ubuf.shape
    rows = pbuf.shape[1]
    piece = samples * block // CHUNKS
    modes = rates_ref.shape[0]
    features = n * width
    me = lax.axis_index("ctx")
    z = lax.axis_index("tp")
    core = rem(me, 2)
    chip = div(me, 2)
    y, x = div(chip, side), rem(chip, side)
    turn = rem(x + y, side)
    sibling = {"ctx": me + 1 - 2 * core}

    def at(yy, xx):
        return {"ctx": 2 * (side * yy + xx) + core}

    def chip_first(q):
        a = div(q, side)
        return side * a + rem(q - side * a + side - a, side)

    def chip_second(q):
        a = div(q, side)
        return side * rem(q - side * a + side - a, side) + a

    def from_last(steps):
        return rem(me + 2 * n - steps, 2 * n)

    quarter = rows // (2 * CHUNKS)
    first_place, second_place = side * y + turn, side * x + turn

    def ring(place, slot, device, chunk):
        return place, slot, chunk, (device(rem(place + 1, n)), device(rem(place + n - 1, n)))

    def first_slot(q):
        return 2 * chip_first(q) + core

    def second_slot(q):
        return 2 * chip_second(q) + core

    rings = [
        ring(z, lambda q: q, lambda q: {"tp": q}, lambda at_slot, c: hraw.at[at_slot, pl.ds(piece * c, piece)]),
        ring(
            first_place, first_slot, lambda q: {"ctx": first_slot(q)},
            lambda at_slot, c: pbuf.at[at_slot, pl.ds(quarter * c, quarter)],
        ),
        ring(
            second_place, second_slot, lambda q: {"ctx": second_slot(q)},
            lambda at_slot, c: pbuf.at[at_slot, pl.ds(rows // 2 + quarter * c, quarter)],
        ),
    ]

    def slot_of(r, way, s):
        place, slot = rings[r][:2]
        return slot(rem(place + n - s, n) if way == RIGHT else rem(place + s, n))

    def ag_copy(r, way, s, c, at_slot):
        part = rings[r][2](at_slot, c)
        return remote(part, part, ag_send.at[r, way, s - 1, c], ag_recv.at[r, way, s - 1, c], rings[r][3][way])

    def ag_start(r, way, s, c, at_slot):
        ag_copy(r, way, s, c, at_slot).start()

    def ag_arrived(r, way, s, c):
        ag_copy(r, way, s, c, 0).wait_recv()

    def ag_sent(r, way, s, c):
        ag_copy(r, way, s, c, 0).wait_send()

    def sib_copy(r, way, s, at_slot):
        part = pbuf.at[at_slot, pl.ds(rows // 2 * (r - 1), rows // 2)]
        return remote(part, part, sib_send.at[r - 1, way, s], sib_recv.at[r - 1, way, s], sibling)

    def sib_wait(r, way, s):
        copy = sib_copy(r, way, s, 0)
        copy.wait_send()
        copy.wait_recv()

    loads = [pltpu.make_async_copy(hid_hbm, hraw.at[z], load_sem.at[0])]
    for j in range(3):
        loads.append(pltpu.make_async_copy(
            w_hbm.at[j], pbuf.at[me, :, pl.ds(width * j, width)], load_sem.at[1 + j]))
    for j in range(2):
        loads.append(pltpu.make_async_copy(
            ow_hbm.at[pl.ds(rows * j, rows)], pbuf.at[me, :, pl.ds(3 * width + rows * j, rows)], load_sem.at[4 + j]))
    small = [(gain_hbm, gain_ref), (taps_hbm, taps_ref), (res_hbm, res_ref), (rates_hbm, rates_ref), (skip_hbm, skip_ref)]
    for j, (source, target) in enumerate(small):
        loads.append(pltpu.make_async_copy(source, target, load_sem.at[6 + j]))
    for copy in loads:
        copy.start()
    partners = [{"tp": rem(z + 1, n)}, {"tp": rem(z + n - 1, n)}, sibling, {"ctx": from_last(1)}]
    for j in range(1, side):
        partners.append(at(y, rem(x + j, side)))
        partners.append(at(rem(y + j, side), x))
    barrier = pltpu.get_barrier_semaphore()
    for partner in partners:
        pl.semaphore_signal(barrier, inc=1, device_id=partner, device_id_type=MESH)
    for copy in loads:
        copy.wait()
    pl.semaphore_wait(barrier, len(partners))

    def take(q):
        gain = gain_ref[:, pl.ds(pl.multiple_of(q * width, width), width)]
        for s in range(samples):
            value = hraw[q, s * block : (s + 1) * block, :].astype(F32)
            span = pl.ds(s * block, block)
            square = value * value
            ssq[span, :] = ssq[span, :] + square[:, : width // 2] + square[:, width // 2 :]
            hs[span, pl.ds(pl.multiple_of(q * width, width), width)] = (value * gain).astype(BF16)

    def goes_far(way, c):
        return (c < CHUNKS // 2) == (way == RIGHT)

    lanes = [(r, way) for r in range(3) for way in (RIGHT, LEFT)]
    mine = [z, me, me]
    for c in range(CHUNKS):
        for r, way in lanes:
            ag_start(r, way, 1, c, mine[r])
    for r in (1, 2):
        sib_copy(r, RIGHT, 0, me).start()
    ssq[...] = jnp.zeros_like(ssq)
    take(z)

    def ag_step(s, carry):
        slots = {(r, way): slot_of(r, way, s) for r, way in lanes}
        for c in range(CHUNKS):
            for r, way in lanes:
                ag_arrived(r, way, s, c)
                ag_start(r, way, s + 1, c, slots[r, way])
        for r, way in lanes[2:]:
            sib_copy(r, way, s, slots[r, way]).start()
        take(slots[0, RIGHT])
        take(slots[0, LEFT])
        return carry

    lax.fori_loop(1, half - 1, ag_step, 0)
    slots = {(r, way): slot_of(r, way, half - 1) for r, way in lanes}
    for c in range(CHUNKS):
        for r, way in lanes:
            ag_arrived(r, way, half - 1, c)
            if goes_far(way, c):
                ag_start(r, way, half, c, slots[r, way])
    for r, way in lanes[2:]:
        sib_copy(r, way, half - 1, slots[r, way]).start()
    take(slots[0, RIGHT])
    take(slots[0, LEFT])
    for r in (1, 2, 0):
        for c in range(CHUNKS):
            ag_arrived(r, RIGHT if goes_far(RIGHT, c) else LEFT, half, c)
        if r:
            sib_copy(r, RIGHT, half, slot_of(r, RIGHT, half)).start()
    take(slot_of(0, RIGHT, half))
    for r in (1, 2):
        sib_wait(r, RIGHT, 0)
        sib_wait(r, RIGHT, half)

    def sib_step(s, carry):
        for r in (1, 2):
            for way in (RIGHT, LEFT):
                sib_wait(r, way, s)
        return carry

    lax.fori_loop(1, half, sib_step, 0)

    deep = 4 if n % 4 == 0 else 1
    span_k = deep * width

    def product(i):
        left = hs[:, pl.ds(pl.multiple_of(i * span_k, span_k), span_k)]
        per = span_k // rows
        right = pbuf[pl.ds(i * per, per), :, : 3 * width].reshape(span_k, 3 * width)
        return jnp.dot(left, right, preferred_element_type=F32)

    acc[...] = product(jnp.int32(0))

    def project(i, carry):
        acc[...] = acc[...] + product(i)
        return carry

    lax.fori_loop(1, n // deep, project, 0)
    mean = jnp.sum(ssq[...], axis=1, keepdims=True) * (1.0 / features)
    scale = lax.rsqrt(mean + 1e-6)
    for s in range(samples):
        ext[s, 8:, :] = acc[s * block : (s + 1) * block, :] * scale[s * block : (s + 1) * block, :]
    rim = remote(ext.at[:, pl.ds(block, 8)], ext.at[:, pl.ds(0, 8)], rim_send, rim_recv, {"ctx": rem(me + 1, 2 * n)})
    rim.start()

    rates = rates_ref[...]
    decay = jnp.exp(-rates)
    whole = jnp.exp(-rates * float(block))
    coef = res_ref[...] * jnp.sqrt(2.0 * rates / modes)

    def powers(place, blocks):
        before, total = [], []
        for i in range(side):
            gap = jnp.maximum(place - 1 - i, 0).astype(F32)
            factor = jnp.exp(-rates * (gap * float(blocks * block)))
            before.append(jnp.where(i < place, factor, 0.0))
            total.append(jnp.exp(-rates * float(blocks * block * (side - 1 - i))))
        return before, total

    def filtered(s, j, first, count):
        total = None
        for i in range(3):
            term = taps_ref[i, j : j + 1, :] * ext[s, 8 + first - i : 8 + first - i + count, j * width : (j + 1) * width]
            total = term if total is None else total + term
        return total

    def features_of(first, count):
        for s in range(samples):
            place = lax.broadcasted_iota(jnp.int32, (count, 1), 0) + (me * block + first)
            valid = jnp.where(place < len_ref[s], 1.0, 0.0)
            span = slice(first, first + count)
            pushed = filtered(s, 1, first, count) * filtered(s, 2, first, count) * valid
            ubuf[s, span, :] = pushed.astype(BF16).astype(F32)
            qbuf[s, span, :] = filtered(s, 0, first, count) * valid

    def gather_state(g, states):
        states = list(states)
        tiles = [ubuf[s, pl.ds(pl.multiple_of(8 * g, 8), 8), :] for s in range(samples)]
        for i in range(8):
            for s in range(samples):
                states[s] = decay * states[s] + tiles[s][i : i + 1, :]
        return tuple(states)

    zero = jnp.zeros((modes, width), F32)
    features_of(8, block - 8)
    ends = lax.fori_loop(1, block // 8, gather_state, (zero,) * samples)
    rim.wait_recv()
    for s in range(samples):
        ext[s, :8, :] = jnp.where(me == 0, 0.0, ext[s, :8, :])
    features_of(0, 8)
    heads = gather_state(0, (zero,) * samples)
    late = jnp.exp(-rates * float(block - 8))
    for s in range(samples):
        st0[core, s] = late * heads[s] + ends[s]
    pair = remote(st0.at[core], st0.at[core], st0_send, st0_recv, sibling)
    pair.start()

    def fill_table(m, carry):
        rate = rates_ref[pl.ds(m, 1), :]
        steps = lax.broadcasted_iota(jnp.int32, (block, 1), 0).astype(F32) + 1.0
        table[m] = res_ref[pl.ds(m, 1), :] * jnp.sqrt(2.0 * rate / modes) * jnp.exp(-rate * steps)
        return carry

    def convolve(s):
        def body(g, state):
            span = pl.ds(pl.multiple_of(8 * g, 8), 8)
            tile = ubuf[s, span, :]
            lines = []
            for i in range(8):
                state = decay * state + tile[i : i + 1, :]
                lines.append(jnp.sum(coef * state, axis=0, keepdims=True))
            cbuf[s, span, :] = jnp.concatenate(lines, axis=0)
            return state

        lax.fori_loop(0, block // 8, body, zero)

    x_before, x_total = powers(x, 2)
    lax.fori_loop(0, modes, fill_table, 0)
    pair_in = remote(st0.at[1 - core], st0.at[1 - core], st0_send, st0_recv, sibling)
    pair_in.wait_recv()
    for s in range(samples):
        st1[x, s] = whole * st0[0, s] + st0[1, s]
    for j in range(1, side):
        remote(st1.at[x], st1.at[x], st1_send.at[j], st1_recv.at[j], at(y, rem(x + j, side))).start()
    y_before, _ = powers(y, 2 * side)
    x_power = jnp.exp(-rates * (x.astype(F32) * float(2 * block)))
    convolve(0)
    for j in range(1, side):
        slot = st1.at[rem(x + side - j, side)]
        remote(slot, slot, st1_send.at[j], st1_recv.at[j], sibling).wait_recv()
    for s in range(samples):
        st2[y, s] = sum(x_total[i] * st1[i, s] for i in range(side))
    for j in range(1, side):
        remote(st2.at[y], st2.at[y], st2_send.at[j], st2_recv.at[j], at(rem(y + j, side), x)).start()
    convolve(1)
    for j in range(1, side):
        slot = st2.at[rem(y + side - j, side)]
        remote(slot, slot, st2_send.at[j], st2_recv.at[j], sibling).wait_recv()
    for s in range(samples):
        row = sum(y_before[i] * st2[i, s] for i in range(side))
        at_chip = x_power * row + sum(x_before[i] * st1[i, s] for i in range(side))
        st_in[s] = jnp.where(core == 0, at_chip, whole * at_chip + st0[0, s])

    tall = 32

    def carry_in(g, carry):
        span = pl.ds(pl.multiple_of(tall * g, tall), tall)
        totals = [cbuf[s, span, :] + skip_ref[...] * ubuf[s, span, :] for s in range(samples)]
        for m in range(modes):
            weight = table[m, span, :]
            for s in range(samples):
                totals[s] = totals[s] + weight * st_in[s, m : m + 1, :]
        for s in range(samples):
            target = pl.ds(pl.multiple_of(block * s + tall * g, tall), tall)
            gated[target, :] = (qbuf[s, span, :] * totals[s]).astype(BF16)
        return carry

    lax.fori_loop(0, block // tall, carry_in, 0)

    def share(d):
        first, second = pbuf[2 * d, :, 3 * width :], pbuf[2 * d + 1, :, 3 * width :]
        right = jnp.concatenate([
            jnp.concatenate([first[:, :rows], second[:, :rows]], axis=1),
            jnp.concatenate([first[:, rows:], second[:, rows:]], axis=1),
        ], axis=0)
        return jnp.dot(gated[...], right, preferred_element_type=F32)

    def rs_copy(way, s, c):
        return remote(
            rs_out.at[way, s - 1, c], rs_in.at[way, s - 1, c],
            rs_send.at[way, s - 1, c], rs_recv.at[way, s - 1, c], rings[0][3][way],
        )

    def prepare(s):
        ahead = half + 1 - s
        parts[RIGHT] = share(rem(z + ahead, n))
        parts[LEFT] = share(rem(z + n - ahead, n))

    def rs_step(s, way, c, first):
        part = parts[way, piece * c : piece * (c + 1), :]
        if not first:
            rs_copy(way, s - 1, c).wait_recv()
            part = part + rs_in[way, s - 2, c].astype(F32)
        rs_out[way, s - 1, c] = part.astype(BF16)
        rs_copy(way, s, c).start()

    order = [(way, c) for far in (False, True) for c in range(CHUNKS) for way in (RIGHT, LEFT) if goes_far(way, c) == far]
    farthest = share(rem(z + half, n))
    for c in range(CHUNKS):
        way = RIGHT if goes_far(RIGHT, c) else LEFT
        rs_out[way, 0, c] = farthest[piece * c : piece * (c + 1), :].astype(BF16)
        rs_copy(way, 1, c).start()
    prepare(2)
    for way, c in order:
        rs_step(2, way, c, not goes_far(way, c))

    def reduce_step(s, carry):
        prepare(s)
        for way, c in order:
            rs_step(s, way, c, False)
        return carry

    lax.fori_loop(3, half + 1, reduce_step, 0)
    own = share(z)
    for c in range(CHUNKS):
        span = slice(piece * c, piece * (c + 1))
        part = own[span, :] + hraw[z, span, :].astype(F32)
        for way in (RIGHT, LEFT):
            rs_copy(way, half, c).wait_recv()
            part = part + rs_in[way, half - 1, c].astype(F32)
        out_ref[span, :] = part.astype(BF16)

    def sent(s, carry):
        for r, way in lanes:
            for c in range(CHUNKS):
                ag_sent(r, way, s, c)
        return carry

    lax.fori_loop(1, half, sent, 0)
    for r, way in lanes:
        for c in range(CHUNKS):
            if goes_far(way, c):
                ag_sent(r, way, half, c)
    rim.wait_send()
    pair.wait_send()
    for j in range(1, side):
        remote(st1.at[x], st1.at[x], st1_send.at[j], st1_recv.at[j], sibling).wait_send()
        remote(st2.at[y], st2.at[y], st2_send.at[j], st2_recv.at[j], sibling).wait_send()

    def reduced(s, carry):
        for way in (RIGHT, LEFT):
            for c in range(CHUNKS):
                rs_copy(way, s, c).wait_send()
        return carry

    lax.fori_loop(2, half + 1, reduced, 0)
    for c in range(CHUNKS):
        rs_copy(RIGHT if goes_far(RIGHT, c) else LEFT, 1, c).wait_send()


def on_device(hidden, norm_gain, in_weight, short_weight, residues, rates, skip_gain, out_weight, lengths):
    samples, block, width = hidden.shape
    rows = in_weight.shape[0]
    n = lax.axis_size("tp")
    side = int(round(n ** 0.5))
    half = n // 2
    modes = rates.shape[0]
    dma = pltpu.SemaphoreType.DMA
    hbm = pl.BlockSpec(memory_space=pltpu.HBM)
    vmem = pl.BlockSpec(memory_space=pltpu.VMEM)
    state = (samples, modes, width)
    return pl.pallas_call(
        functools.partial(kernel, side),
        out_shape=jax.ShapeDtypeStruct((samples * block, width), BF16),
        in_specs=[hbm] * 8 + [pl.BlockSpec(memory_space=pltpu.SMEM)],
        out_specs=vmem,
        scratch_shapes=[
            pltpu.VMEM((1, n * width), F32),
            pltpu.VMEM(short_weight.shape, F32),
            pltpu.VMEM(rates.shape, F32),
            pltpu.VMEM(rates.shape, F32),
            pltpu.VMEM((1, width), F32),
            pltpu.VMEM((n, samples * block, width), BF16),
            pltpu.VMEM((samples * block, n * width), BF16),
            pltpu.VMEM((2 * n, rows, 3 * width + 2 * rows), BF16),
            pltpu.VMEM((samples * block, width // 2), F32),
            pltpu.VMEM((samples * block, 3 * width), F32),
            pltpu.VMEM((samples, block + 8, 3 * width), F32),
            pltpu.VMEM((samples, block, width), F32),
            pltpu.VMEM((samples, block, width), F32),
            pltpu.VMEM((samples, block, width), F32),
            pltpu.VMEM((samples * block, width), BF16),
            pltpu.VMEM((modes, block, width), F32),
            pltpu.VMEM(state, F32),
            pltpu.VMEM((2,) + state, F32),
            pltpu.VMEM((side,) + state, F32),
            pltpu.VMEM((side,) + state, F32),
            pltpu.VMEM((2, samples * block, width), F32),
            pltpu.VMEM((2, half, CHUNKS, samples * block // CHUNKS, width), BF16),
            pltpu.VMEM((2, half, CHUNKS, samples * block // CHUNKS, width), BF16),
            dma((11,)),
            dma((3, 2, half, CHUNKS)),
            dma((3, 2, half, CHUNKS)),
            dma((2, 2, half + 1)),
            dma((2, 2, half + 1)),
            dma,
            dma,
            dma,
            dma,
            dma((side,)),
            dma((side,)),
            dma((side,)),
            dma((side,)),
            dma((2, half, CHUNKS)),
            dma((2, half, CHUNKS)),
        ],
        compiler_params=pltpu.CompilerParams(
            collective_id=0, has_side_effects=True, vmem_limit_bytes=60 * 2**20
        ),
    )(
        hidden.reshape(samples * block, width),
        jnp.transpose(in_weight, (1, 0, 2)),
        out_weight,
        norm_gain.reshape(1, n * width),
        short_weight,
        residues,
        rates,
        skip_gain.reshape(1, width),
        lengths,
    ).reshape(hidden.shape)


def solution(mesh):
    placed = (
        P(None, "ctx", "tp"),
        P(),
        P("ctx", None, "tp"),
        P(None, None, "tp"),
        P(None, "tp"),
        P(None, "tp"),
        P("tp"),
        P("tp", "ctx"),
        P(),
    )
    return jax.shard_map(
        on_device, mesh=mesh, in_specs=placed, out_specs=P(None, "ctx", "tp"), check_vma=False
    )
```

time: 105 us -> 98.6 us (0.939)
  local copies, waits for them, and re-layouts: 4.76 us -> 1.57 us
  Pallas kernels: 98.7 us -> 96.4 us
    unnamed x17 -> x1, local copies, waits for them, and re-layouts: 4.01 us -> 1.57 us
    pallas_call x1, Pallas kernels: 98.7 us -> 96.4 us  [on_device(): pl.pallas_call(functools.partial(kernel, side), out_shape=jax.ShapeDtypeS...]
where the time goes in v2:
time: 98.6 us; the launch traced here: 98 us
  Pallas kernels  96.4 us (98%)
  local copies, waits for them, and re-layouts  1.57 us (2%)
    pallas_call x1, Pallas kernels, on_device(): pl.pallas_call(functools.partial(kernel, side), out_shape=jax.ShapeDtypeS...  96.4 us

profile of v2, /device:TPU:6, one launch (start us, length us, event | category | flops | bytes accessed | tf_op | source)
XLA Modules:
  0.0 98.0 jit_solution(16854621699912836647)
XLA Ops:
  0.0 96.4 %shard_map.91 = bf16[256,256]{1,0:T(8,128)(2,1)} custom-call(bf16[256,256]{1,0:T(8,128)(2,1)} %bitcast.7, bf16[3,128,256]{2,1,0:T(8,128)(2,1)} %bitcast.6, bf16[256,128]{1,0:T(8,128)(2,1)} %ow_hbm.1, f32[1,4096]{1,0:T(1,128)} %bitcast.8, f32[3,3,256]{2,1,0:T(4,128)} %taps_hbm.1, f32[16,256]{1,0:T(8,128)} %res_hbm.1, f32[16,256]{1,0:T(8,128)} %rates_hbm.1, ...), custom_call_target="tpu_custom_call" | custom-call | tf_op jit(solution)/shard_map/pallas_call | solution.py:432
  96.4 1.6 %copy.11 = bf16[2,128,256]{2,1,0:T(8,128)(2,1)} copy(bf16[2,128,256]{2,1,0:T(8,128)(2,1)} %bitcast.5) | data formatting | bytes 262144

commit v3 on v2

--- a/solution.py
+++ b/solution.py
@@ -31,7 +31,7 @@
 def kernel(
     side, hid_hbm, w_hbm, ow_hbm, gain_hbm, taps_hbm, res_hbm, rates_hbm, skip_hbm, len_ref, out_ref,
     gain_ref, taps_ref, res_ref, rates_ref, skip_ref,
-    hraw, hs, pbuf, ssq, acc, ext, qbuf, ubuf, cbuf, gated, table, st_in, st0, st1, st2, parts, rs_out, rs_in,
+    hraw, hs, pbuf, ssq, acc, ext, qbuf, ubuf, cbuf, gated, table, st_in, st0, st1, st2, parts, own, rs_out, rs_in,
     load_sem, ag_send, ag_recv, sib_send, sib_recv, rim_send, rim_recv,
     st0_send, st0_recv, st1_send, st1_recv, st2_send, st2_recv, rs_send, rs_recv,
 ):
@@ -151,9 +151,10 @@
 
     lanes = [(r, way) for r in range(3) for way in (RIGHT, LEFT)]
     mine = [z, me, me]
-    for c in range(CHUNKS):
-        for r, way in lanes:
-            ag_start(r, way, 1, c, mine[r])
+    chunks = [(0, way, c) for c in range(CHUNKS) for way in (RIGHT, LEFT)]
+    chunks += [(r, way, c) for c in range(CHUNKS) for r, way in lanes[2:]]
+    for r, way, c in chunks:
+        ag_start(r, way, 1, c, mine[r])
     for r in (1, 2):
         sib_copy(r, RIGHT, 0, me).start()
     ssq[...] = jnp.zeros_like(ssq)
@@ -161,10 +162,9 @@
 
     def ag_step(s, carry):
         slots = {(r, way): slot_of(r, way, s) for r, way in lanes}
-        for c in range(CHUNKS):
-            for r, way in lanes:
-                ag_arrived(r, way, s, c)
-                ag_start(r, way, s + 1, c, slots[r, way])
+        for r, way, c in chunks:
+            ag_arrived(r, way, s, c)
+            ag_start(r, way, s + 1, c, slots[r, way])
         for r, way in lanes[2:]:
             sib_copy(r, way, s, slots[r, way]).start()
         take(slots[0, RIGHT])
@@ -173,11 +173,10 @@
 
     lax.fori_loop(1, half - 1, ag_step, 0)
     slots = {(r, way): slot_of(r, way, half - 1) for r, way in lanes}
-    for c in range(CHUNKS):
-        for r, way in lanes:
-            ag_arrived(r, way, half - 1, c)
-            if goes_far(way, c):
-                ag_start(r, way, half, c, slots[r, way])
+    for r, way, c in chunks:
+        ag_arrived(r, way, half - 1, c)
+        if goes_far(way, c):
+            ag_start(r, way, half, c, slots[r, way])
     for r, way in lanes[2:]:
         sib_copy(r, way, half - 1, slots[r, way]).start()
     take(slots[0, RIGHT])
@@ -294,6 +293,12 @@
 
         lax.fori_loop(0, block // 8, body, zero)
 
+    def sent(s, carry):
+        for r, way in lanes:
+            for c in range(CHUNKS):
+                ag_sent(r, way, s, c)
+        return carry
+
     x_before, x_total = powers(x, 2)
     lax.fori_loop(0, modes, fill_table, 0)
     pair_in = remote(st0.at[1 - core], st0.at[1 - core], st0_send, st0_recv, sibling)
@@ -305,6 +310,7 @@
     y_before, _ = powers(y, 2 * side)
     x_power = jnp.exp(-rates * (x.astype(F32) * float(2 * block)))
     convolve(0)
+    lax.fori_loop(1, half // 2, sent, 0)
     for j in range(1, side):
         slot = st1.at[rem(x + side - j, side)]
         remote(slot, slot, st1_send.at[j], st1_recv.at[j], sibling).wait_recv()
@@ -313,6 +319,11 @@
     for j in range(1, side):
         remote(st2.at[y], st2.at[y], st2_send.at[j], st2_recv.at[j], at(rem(y + j, side), x)).start()
     convolve(1)
+    lax.fori_loop(half // 2, half, sent, 0)
+    for r, way in lanes:
+        for c in range(CHUNKS):
+            if goes_far(way, c):
+                ag_sent(r, way, half, c)
     for j in range(1, side):
         slot = st2.at[rem(y + side - j, side)]
         remote(slot, slot, st2_send.at[j], st2_recv.at[j], sibling).wait_recv()
@@ -371,51 +382,40 @@
         rs_out[way, 0, c] = farthest[piece * c : piece * (c + 1), :].astype(BF16)
         rs_copy(way, 1, c).start()
     prepare(2)
+    own[...] = share(z) + hraw[z].astype(F32)
     for way, c in order:
         rs_step(2, way, c, not goes_far(way, c))
 
+    for c in range(CHUNKS):
+        rs_copy(RIGHT if goes_far(RIGHT, c) else LEFT, 1, c).wait_send()
+
+    def rs_sent(s):
+        for way in (RIGHT, LEFT):
+            for c in range(CHUNKS):
+                rs_copy(way, s, c).wait_send()
+
     def reduce_step(s, carry):
         prepare(s)
+        rs_sent(s - 1)
         for way, c in order:
             rs_step(s, way, c, False)
         return carry
 
     lax.fori_loop(3, half + 1, reduce_step, 0)
-    own = share(z)
     for c in range(CHUNKS):
         span = slice(piece * c, piece * (c + 1))
-        part = own[span, :] + hraw[z, span, :].astype(F32)
+        part = own[span, :]
         for way in (RIGHT, LEFT):
             rs_copy(way, half, c).wait_recv()
             part = part + rs_in[way, half - 1, c].astype(F32)
         out_ref[span, :] = part.astype(BF16)
 
-    def sent(s, carry):
-        for r, way in lanes:
-            for c in range(CHUNKS):
-                ag_sent(r, way, s, c)
-        return carry
-
-    lax.fori_loop(1, half, sent, 0)
-    for r, way in lanes:
-        for c in range(CHUNKS):
-            if goes_far(way, c):
-                ag_sent(r, way, half, c)
     rim.wait_send()
     pair.wait_send()
     for j in range(1, side):
         remote(st1.at[x], st1.at[x], st1_send.at[j], st1_recv.at[j], sibling).wait_send()
         remote(st2.at[y], st2.at[y], st2_send.at[j], st2_recv.at[j], sibling).wait_send()
-
-    def reduced(s, carry):
-        for way in (RIGHT, LEFT):
-            for c in range(CHUNKS):
-                rs_copy(way, s, c).wait_send()
-        return carry
-
-    lax.fori_loop(2, half + 1, reduced, 0)
-    for c in range(CHUNKS):
-        rs_copy(RIGHT if goes_far(RIGHT, c) else LEFT, 1, c).wait_send()
+    rs_sent(half)
 
 
 def on_device(hidden, norm_gain, in_weight, short_weight, residues, rates, skip_gain, out_weight, lengths):
@@ -456,6 +456,7 @@
             pltpu.VMEM((side,) + state, F32),
             pltpu.VMEM((side,) + state, F32),
             pltpu.VMEM((2, samples * block, width), F32),
+            pltpu.VMEM((samples * block, width), F32),
             pltpu.VMEM((2, half, CHUNKS, samples * block // CHUNKS, width), BF16),
             pltpu.VMEM((2, half, CHUNKS, samples * block // CHUNKS, width), BF16),
             dma((11,)),

time: 98.6 us -> 101 us (1.024)
  Pallas kernels: 96.4 us -> 98.3 us
    pallas_call x1, Pallas kernels: 96.4 us -> 98.3 us  [on_device(): pl.pallas_call(functools.partial(kernel, side), out_shape=jax.ShapeDtypeS...]
where the time goes in v3:
time: 101 us; the launch traced here: 99.9 us
  Pallas kernels  98.3 us (97%)
  local copies, waits for them, and re-layouts  1.57 us (2%)
    pallas_call x1, Pallas kernels, on_device(): pl.pallas_call(functools.partial(kernel, side), out_shape=jax.ShapeDtypeS...  98.3 us

profile of v3, /device:TPU:6, one launch (start us, length us, event | category | flops | bytes accessed | tf_op | source)
XLA Modules:
  0.0 99.9 jit_solution(16434841854007068768)
XLA Ops:
  0.0 98.3 %shard_map.91 = bf16[256,256]{1,0:T(8,128)(2,1)} custom-call(bf16[256,256]{1,0:T(8,128)(2,1)} %bitcast.7, bf16[3,128,256]{2,1,0:T(8,128)(2,1)} %bitcast.6, bf16[256,128]{1,0:T(8,128)(2,1)} %ow_hbm.1, f32[1,4096]{1,0:T(1,128)} %bitcast.8, f32[3,3,256]{2,1,0:T(4,128)} %taps_hbm.1, f32[16,256]{1,0:T(8,128)} %res_hbm.1, f32[16,256]{1,0:T(8,128)} %rates_hbm.1, ...), custom_call_target="tpu_custom_call" | custom-call | tf_op jit(solution)/shard_map/pallas_call | solution.py:432
  98.4 1.6 %copy.11 = bf16[2,128,256]{2,1,0:T(8,128)(2,1)} copy(bf16[2,128,256]{2,1,0:T(8,128)(2,1)} %bitcast.5) | data formatting | bytes 262144

commit v4 on v2

v4 whole, which is shorter than its diff:
```python
import functools

import jax
import jax.numpy as jnp
from jax import lax
from jax.experimental import pallas as pl
from jax.experimental.pallas import tpu as pltpu
from jax.sharding import PartitionSpec as P

MESH = pl.DeviceIdType.MESH
F32, BF16 = jnp.float32, jnp.bfloat16
RIGHT, LEFT = 0, 1
CHUNKS = 4


def rem(a, b):
    return lax.rem(a, jnp.int32(b))


def div(a, b):
    return lax.div(a, jnp.int32(b))


def remote(src, dst, send_sem, recv_sem, device):
    return pltpu.make_async_remote_copy(
        src_ref=src, dst_ref=dst, send_sem=send_sem, recv_sem=recv_sem,
        device_id=device, device_id_type=MESH,
    )


def kernel(
    side, hid_hbm, w_hbm, ow_hbm, gain_hbm, taps_hbm, res_hbm, rates_hbm, skip_hbm, len_ref, out_ref,
    gain_ref, taps_ref, res_ref, rates_ref, skip_ref,
    hraw, hs, pbuf, ssq, acc, ext, qbuf, ubuf, cbuf, gated, table, st_in, st0, st1, st2, parts, rs_out, rs_in,
    load_sem, ag_send, ag_recv, sib_send, sib_recv, rim_send, rim_recv,
    st0_send, st0_recv, st1_send, st1_recv, st2_send, st2_recv, rs_send, rs_recv,
):
    n = side * side
    half = n // 2
    samples, block, width = ubuf.shape
    rows = pbuf.shape[1]
    piece = samples * block // CHUNKS
    modes = rates_ref.shape[0]
    features = n * width
    me = lax.axis_index("ctx")
    z = lax.axis_index("tp")
    core = rem(me, 2)
    chip = div(me, 2)
    y, x = div(chip, side), rem(chip, side)
    turn = rem(x + y, side)
    sibling = {"ctx": me + 1 - 2 * core}

    def at(yy, xx):
        return {"ctx": 2 * (side * yy + xx) + core}

    def chip_first(q):
        a = div(q, side)
        return side * a + rem(q - side * a + side - a, side)

    def chip_second(q):
        a = div(q, side)
        return side * rem(q - side * a + side - a, side) + a

    def from_last(steps):
        return rem(me + 2 * n - steps, 2 * n)

    quarter = rows // CHUNKS
    columns = (pl.ds(0, 3 * width), pl.ds(3 * width, 2 * rows))

    first_place, second_place = side * y + turn, side * x + turn

    def ring(place, slot, device, chunk):
        return place, slot, chunk, (device(rem(place + 1, n)), device(rem(place + n - 1, n)))

    def first_slot(q):
        return 2 * chip_first(q) + core

    def second_slot(q):
        return 2 * chip_second(q) + core

    rings = [
        ring(z, lambda q: q, lambda q: {"tp": q}, lambda at_slot, c: hraw.at[at_slot, pl.ds(piece * c, piece)]),
        ring(
            first_place, first_slot, lambda q: {"ctx": first_slot(q)},
            lambda at_slot, c: pbuf.at[at_slot, pl.ds(quarter * (c % 2), quarter), columns[c // 2]],
        ),
        ring(
            second_place, second_slot, lambda q: {"ctx": second_slot(q)},
            lambda at_slot, c: pbuf.at[at_slot, pl.ds(rows // 2 + quarter * (c % 2), quarter), columns[c // 2]],
        ),
    ]

    def slot_of(r, way, s):
        place, slot = rings[r][:2]
        return slot(rem(place + n - s, n) if way == RIGHT else rem(place + s, n))

    def ag_copy(r, way, s, c, at_slot):
        part = rings[r][2](at_slot, c)
        return remote(part, part, ag_send.at[r, way, s - 1, c], ag_recv.at[r, way, s - 1, c], rings[r][3][way])

    def ag_start(r, way, s, c, at_slot):
        ag_copy(r, way, s, c, at_slot).start()

    def ag_arrived(r, way, s, c):
        ag_copy(r, way, s, c, 0).wait_recv()

    def ag_sent(r, way, s, c):
        ag_copy(r, way, s, c, 0).wait_send()

    def sib_copy(phase, r, way, s, at_slot):
        part = pbuf.at[at_slot, pl.ds(rows // 2 * (r - 1), rows // 2), columns[phase]]
        return remote(part, part, sib_send.at[phase, r - 1, way, s], sib_recv.at[phase, r - 1, way, s], sibling)

    def sib_wait(phase, r, way, s):
        copy = sib_copy(phase, r, way, s, 0)
        copy.wait_send()
        copy.wait_recv()

    loads = [pltpu.make_async_copy(hid_hbm, hraw.at[z], load_sem.at[0])]
    for j in range(3):
        loads.append(pltpu.make_async_copy(
            w_hbm.at[j], pbuf.at[me, :, pl.ds(width * j, width)], load_sem.at[1 + j]))
    for j in range(2):
        loads.append(pltpu.make_async_copy(
            ow_hbm.at[pl.ds(rows * j, rows)], pbuf.at[me, :, pl.ds(3 * width + rows * j, rows)], load_sem.at[4 + j]))
    small = [(gain_hbm, gain_ref), (taps_hbm, taps_ref), (res_hbm, res_ref), (rates_hbm, rates_ref), (skip_hbm, skip_ref)]
    for j, (source, target) in enumerate(small):
        loads.append(pltpu.make_async_copy(source, target, load_sem.at[6 + j]))
    for copy in loads:
        copy.start()
    partners = [{"tp": rem(z + 1, n)}, {"tp": rem(z + n - 1, n)}, sibling, {"ctx": from_last(1)}]
    for j in range(1, side):
        partners.append(at(y, rem(x + j, side)))
        partners.append(at(rem(y + j, side), x))
    barrier = pltpu.get_barrier_semaphore()
    for partner in partners:
        pl.semaphore_signal(barrier, inc=1, device_id=partner, device_id_type=MESH)
    for copy in loads:
        copy.wait()
    pl.semaphore_wait(barrier, len(partners))

    def take(q, s):
        gain = gain_ref[:, pl.ds(pl.multiple_of(q * width, width), width)]
        span = pl.ds(s * block, block)
        value = hraw[q, span, :].astype(F32)
        square = value * value
        ssq[span, :] = ssq[span, :] + square[:, : width // 2] + square[:, width // 2 :]
        hs[span, pl.ds(pl.multiple_of(q * width, width), width)] = (value * gain).astype(BF16)

    def goes_far(way, c):
        return (c % 2 == 0) == (way == RIGHT)

    lanes = [(r, way) for r in range(3) for way in (RIGHT, LEFT)]
    mine = [z, me, me]

    def ag_begin(phase):
        for c in (2 * phase, 2 * phase + 1):
            for r, way in lanes:
                ag_start(r, way, 1, c, mine[r])

    def ag_step(phase, s, last):
        slots = {(r, way): slot_of(r, way, s) for r, way in lanes}
        for c in (2 * phase, 2 * phase + 1):
            for r, way in lanes:
                ag_arrived(r, way, s, c)
                if not last or goes_far(way, c):
                    ag_start(r, way, s + 1, c, slots[r, way])
        for r, way in lanes[2:]:
            sib_copy(phase, r, way, s, slots[r, way]).start()
        take(slots[0, RIGHT], phase)
        take(slots[0, LEFT], phase)

    def ag_end(phase):
        for r in (1, 2, 0):
            for c in (2 * phase, 2 * phase + 1):
                ag_arrived(r, RIGHT if goes_far(RIGHT, c) else LEFT, half, c)
            if r:
                sib_copy(phase, r, RIGHT, half, slot_of(r, RIGHT, half)).start()
        take(slot_of(0, RIGHT, half), phase)

    def sib_end(phase):
        def step(s, carry):
            for r in (1, 2):
                for way in (RIGHT, LEFT):
                    sib_wait(phase, r, way, s)
            return carry

        lax.fori_loop(1, half, step, 0)
        for r in (1, 2):
            sib_wait(phase, r, RIGHT, 0)
            sib_wait(phase, r, RIGHT, half)

    ag_begin(0)
    for phase in range(2):
        for r in (1, 2):
            sib_copy(phase, r, RIGHT, 0, me).start()
    ssq[...] = jnp.zeros_like(ssq)
    take(z, 0)
    take(z, 1)

    def first_phase(s, carry):
        ag_step(0, s, False)
        return carry

    lax.fori_loop(1, half - 1, first_phase, 0)
    ag_step(0, half - 1, True)
    ag_begin(1)
    ag_end(0)
    sib_end(0)

    deep = 4 if n % 4 == 0 else 1
    span_k = deep * width

    def project(s, i):
        span = pl.ds(s * block, block)
        per = span_k // rows
        left = hs[span, i * span_k : (i + 1) * span_k]
        right = pbuf[i * per : (i + 1) * per, :, : 3 * width].reshape(span_k, 3 * width)
        product = jnp.dot(left, right, preferred_element_type=F32)
        acc[span, :] = product if i == 0 else acc[span, :] + product

    def rim_copy(s):
        return remote(
            ext.at[s, pl.ds(block, 8)], ext.at[s, pl.ds(0, 8)], rim_send.at[s], rim_recv.at[s],
            {"ctx": rem(me + 1, 2 * n)},
        )

    def normalize(s):
        span = pl.ds(s * block, block)
        mean = jnp.sum(ssq[span, :], axis=1, keepdims=True) * (1.0 / features)
        ext[s, 8:, :] = acc[span, :] * lax.rsqrt(mean + 1e-6)
        rim_copy(s).start()

    rates = rates_ref[...]
    decay = jnp.exp(-rates)
    whole = jnp.exp(-rates * float(block))
    coef = res_ref[...] * jnp.sqrt(2.0 * rates / modes)

    def powers(place, blocks):
        before, total = [], []
        for i in range(side):
            gap = jnp.maximum(place - 1 - i, 0).astype(F32)
            factor = jnp.exp(-rates * (gap * float(blocks * block)))
            before.append(jnp.where(i < place, factor, 0.0))
            total.append(jnp.exp(-rates * float(blocks * block * (side - 1 - i))))
        return before, total

    def filtered(s, j, first, count):
        total = None
        for i in range(3):
            term = taps_ref[i, j : j + 1, :] * ext[s, 8 + first - i : 8 + first - i + count, j * width : (j + 1) * width]
            total = term if total is None else total + term
        return total

    def features_of(s, first, count):
        place = lax.broadcasted_iota(jnp.int32, (count, 1), 0) + (me * block + first)
        valid = jnp.where(place < len_ref[s], 1.0, 0.0)
        span = slice(first, first + count)
        pushed = filtered(s, 1, first, count) * filtered(s, 2, first, count) * valid
        ubuf[s, span, :] = pushed.astype(BF16).astype(F32)
        qbuf[s, span, :] = filtered(s, 0, first, count) * valid

    zero = jnp.zeros((modes, width), F32)

    def add_states(s, first, last):
        def body(g, state):
            tile = ubuf[s, pl.ds(pl.multiple_of(8 * g, 8), 8), :]
            for i in range(8):
                state = decay * state + tile[i : i + 1, :]
            return state

        return lax.fori_loop(first, last, body, zero)

    def pair_copy(s, which):
        return remote(st0.at[which, s], st0.at[which, s], st0_send.at[s], st0_recv.at[s], sibling)

    def x_copy(s, j, slot, to):
        return remote(st1.at[slot, s], st1.at[slot, s], st1_send.at[s, j], st1_recv.at[s, j], to)

    def y_copy(s, j, slot, to):
        return remote(st2.at[slot, s], st2.at[slot, s], st2_send.at[s, j], st2_recv.at[s, j], to)

    def tail_state(s):
        features_of(s, 8, block - 8)
        st_in[s] = add_states(s, 1, block // 8)

    def end_state(s):
        rim_copy(s).wait_recv()
        ext[s, :8, :] = jnp.where(me == 0, 0.0, ext[s, :8, :])
        features_of(s, 0, 8)
        st0[core, s] = jnp.exp(-rates * float(block - 8)) * add_states(s, 0, 1) + st_in[s]
        pair_copy(s, core).start()

    def fill_table():
        def body(m, carry):
            rate = rates_ref[pl.ds(m, 1), :]
            steps = lax.broadcasted_iota(jnp.int32, (block, 1), 0).astype(F32) + 1.0
            table[m] = res_ref[pl.ds(m, 1), :] * jnp.sqrt(2.0 * rate / modes) * jnp.exp(-rate * steps)
            return carry

        lax.fori_loop(0, modes, body, 0)

    def convolve(s):
        def body(g, state):
            span = pl.ds(pl.multiple_of(8 * g, 8), 8)
            tile = ubuf[s, span, :]
            lines = []
            for i in range(8):
                state = decay * state + tile[i : i + 1, :]
                lines.append(jnp.sum(coef * state, axis=0, keepdims=True))
            cbuf[s, span, :] = jnp.concatenate(lines, axis=0)
            return state

        lax.fori_loop(0, block // 8, body, zero)

    def to_row(s):
        pair_copy(s, 1 - core).wait_recv()
        st1[x, s] = whole * st0[0, s] + st0[1, s]
        for j in range(1, side):
            x_copy(s, j, x, at(y, rem(x + j, side))).start()

    def to_column(s):
        for j in range(1, side):
            x_copy(s, j, rem(x + side - j, side), sibling).wait_recv()
        _, x_total = powers(x, 2)
        st2[y, s] = sum(x_total[i] * st1[i, s] for i in range(side))
        for j in range(1, side):
            y_copy(s, j, y, at(rem(y + j, side), x)).start()

    tall = 32

    def gate(s):
        x_before, _ = powers(x, 2)
        y_before, _ = powers(y, 2 * side)
        x_power = jnp.exp(-rates * (x.astype(F32) * float(2 * block)))
        for j in range(1, side):
            y_copy(s, j, rem(y + side - j, side), sibling).wait_recv()
        row = sum(y_before[i] * st2[i, s] for i in range(side))
        at_chip = x_power * row + sum(x_before[i] * st1[i, s] for i in range(side))
        st_in[s] = jnp.where(core == 0, at_chip, whole * at_chip + st0[0, s])

        def body(g, carry):
            span = pl.ds(pl.multiple_of(tall * g, tall), tall)
            total = cbuf[s, span, :] + skip_ref[...] * ubuf[s, span, :]
            for m in range(modes):
                total = total + table[m, span, :] * st_in[s, m : m + 1, :]
            target = pl.ds(pl.multiple_of(block * s + tall * g, tall), tall)
            gated[target, :] = (qbuf[s, span, :] * total).astype(BF16)
            return carry

        lax.fori_loop(0, block // tall, body, 0)

    def share(d, s):
        first, second = pbuf[2 * d, :, 3 * width :], pbuf[2 * d + 1, :, 3 * width :]
        right = jnp.concatenate([
            jnp.concatenate([first[:, :rows], second[:, :rows]], axis=1),
            jnp.concatenate([first[:, rows:], second[:, rows:]], axis=1),
        ], axis=0)
        return jnp.dot(gated[block * s : block * (s + 1), :], right, preferred_element_type=F32)

    def rs_copy(way, s, c):
        return remote(
            rs_out.at[way, s - 1, c], rs_in.at[way, s - 1, c],
            rs_send.at[way, s - 1, c], rs_recv.at[way, s - 1, c], rings[0][3][way],
        )

    def prepare(sample, s):
        ahead = half + 1 - s
        span = slice(block * sample, block * (sample + 1))
        parts[RIGHT, span, :] = share(rem(z + ahead, n), sample)
        parts[LEFT, span, :] = share(rem(z + n - ahead, n), sample)

    def rs_send_on(s, way, c, first):
        part = parts[way, piece * c : piece * (c + 1), :]
        if not first:
            rs_copy(way, s - 1, c).wait_recv()
            part = part + rs_in[way, s - 2, c].astype(F32)
        rs_out[way, s - 1, c] = part.astype(BF16)
        rs_copy(way, s, c).start()

    def order(sample):
        return [(RIGHT, 2 * sample + 1), (LEFT, 2 * sample), (RIGHT, 2 * sample), (LEFT, 2 * sample + 1)]

    def rs_begin(sample):
        farthest = share(rem(z + half, n), sample)
        for i, way in enumerate((RIGHT, LEFT)):
            c = 2 * sample + i
            rs_out[way, 0, c] = farthest[piece * i : piece * (i + 1), :].astype(BF16)
            rs_copy(way, 1, c).start()
        prepare(sample, 2)
        for way, c in order(sample):
            rs_send_on(2, way, c, not goes_far(way, c))

    def rs_step(sample, s):
        prepare(sample, s)
        for way, c in order(sample):
            rs_send_on(s, way, c, False)

    def rs_end(sample):
        own = share(z, sample)
        for i in range(2):
            c = 2 * sample + i
            span = slice(piece * c, piece * (c + 1))
            part = own[piece * i : piece * (i + 1), :] + hraw[z, span, :].astype(F32)
            for way in (RIGHT, LEFT):
                rs_copy(way, half, c).wait_recv()
                part = part + rs_in[way, half - 1, c].astype(F32)
            out_ref[span, :] = part.astype(BF16)

    def work(s):
        def run(f, *more):
            return lambda: f(s, *more)

        jobs = [run(project, i) for i in range(n // deep)]
        jobs += [run(normalize), run(tail_state), run(end_state)]
        jobs += [fill_table] if s == 0 else []
        return jobs + [run(to_row), run(convolve), run(to_column), run(gate)]

    def interleave(jobs, steps):
        for i in range(max(len(jobs), len(steps))):
            if i < len(jobs):
                jobs[i]()
            if i < len(steps):
                steps[i]()

    steps = [functools.partial(ag_step, 1, s, s == half - 1) for s in range(1, half)] + [lambda: ag_end(1)]
    interleave(work(0), steps)
    sib_end(1)
    rs_begin(0)
    interleave(work(1), [functools.partial(rs_step, 0, s) for s in range(3, half + 1)])
    rs_begin(1)
    rs_end(0)

    def reduce_step(s, carry):
        rs_step(1, s)
        return carry

    lax.fori_loop(3, half + 1, reduce_step, 0)
    rs_end(1)

    def sent(s, carry):
        for r, way in lanes:
            for c in range(CHUNKS):
                ag_sent(r, way, s, c)
        return carry

    lax.fori_loop(1, half, sent, 0)
    for r, way in lanes:
        for c in range(CHUNKS):
            if goes_far(way, c):
                ag_sent(r, way, half, c)
    for s in range(samples):
        rim_copy(s).wait_send()
        pair_copy(s, core).wait_send()
        for j in range(1, side):
            x_copy(s, j, x, sibling).wait_send()
            y_copy(s, j, y, sibling).wait_send()

    def reduced(s, carry):
        for way in (RIGHT, LEFT):
            for c in range(CHUNKS):
                rs_copy(way, s, c).wait_send()
        return carry

    lax.fori_loop(2, half + 1, reduced, 0)
    for c in range(CHUNKS):
        rs_copy(RIGHT if goes_far(RIGHT, c) else LEFT, 1, c).wait_send()


def on_device(hidden, norm_gain, in_weight, short_weight, residues, rates, skip_gain, out_weight, lengths):
    samples, block, width = hidden.shape
    rows = in_weight.shape[0]
    n = lax.axis_size("tp")
    side = int(round(n ** 0.5))
    half = n // 2
    modes = rates.shape[0]
    dma = pltpu.SemaphoreType.DMA
    hbm = pl.BlockSpec(memory_space=pltpu.HBM)
    vmem = pl.BlockSpec(memory_space=pltpu.VMEM)
    state = (samples, modes, width)
    return pl.pallas_call(
        functools.partial(kernel, side),
        out_shape=jax.ShapeDtypeStruct((samples * block, width), BF16),
        in_specs=[hbm] * 8 + [pl.BlockSpec(memory_space=pltpu.SMEM)],
        out_specs=vmem,
        scratch_shapes=[
            pltpu.VMEM((1, n * width), F32),
            pltpu.VMEM(short_weight.shape, F32),
            pltpu.VMEM(rates.shape, F32),
            pltpu.VMEM(rates.shape, F32),
            pltpu.VMEM((1, width), F32),
            pltpu.VMEM((n, samples * block, width), BF16),
            pltpu.VMEM((samples * block, n * width), BF16),
            pltpu.VMEM((2 * n, rows, 3 * width + 2 * rows), BF16),
            pltpu.VMEM((samples * block, width // 2), F32),
            pltpu.VMEM((samples * block, 3 * width), F32),
            pltpu.VMEM((samples, block + 8, 3 * width), F32),
            pltpu.VMEM((samples, block, width), F32),
            pltpu.VMEM((samples, block, width), F32),
            pltpu.VMEM((samples, block, width), F32),
            pltpu.VMEM((samples * block, width), BF16),
            pltpu.VMEM((modes, block, width), F32),
            pltpu.VMEM(state, F32),
            pltpu.VMEM((2,) + state, F32),
            pltpu.VMEM((side,) + state, F32),
            pltpu.VMEM((side,) + state, F32),
            pltpu.VMEM((2, samples * block, width), F32),
            pltpu.VMEM((2, half, CHUNKS, samples * block // CHUNKS, width), BF16),
            pltpu.VMEM((2, half, CHUNKS, samples * block // CHUNKS, width), BF16),
            dma((11,)),
            dma((3, 2, half, CHUNKS)),
            dma((3, 2, half, CHUNKS)),
            dma((2, 2, 2, half + 1)),
            dma((2, 2, 2, half + 1)),
            dma((samples,)),
            dma((samples,)),
            dma((samples,)),
            dma((samples,)),
            dma((samples, side)),
            dma((samples, side)),
            dma((samples, side)),
            dma((samples, side)),
            dma((2, half, CHUNKS)),
            dma((2, half, CHUNKS)),
        ],
        compiler_params=pltpu.CompilerParams(
            collective_id=0, has_side_effects=True, vmem_limit_bytes=60 * 2**20
        ),
    )(
        hidden.reshape(samples * block, width),
        jnp.transpose(in_weight, (1, 0, 2)),
        out_weight,
        norm_gain.reshape(1, n * width),
        short_weight,
        residues,
        rates,
        skip_gain.reshape(1, width),
        lengths,
    ).reshape(hidden.shape)


def solution(mesh):
    placed = (
        P(None, "ctx", "tp"),
        P(),
        P("ctx", None, "tp"),
        P(None, None, "tp"),
        P(None, "tp"),
        P(None, "tp"),
        P("tp"),
        P("tp", "ctx"),
        P(),
    )
    return jax.shard_map(
        on_device, mesh=mesh, in_specs=placed, out_specs=P(None, "ctx", "tp"), check_vma=False
    )
```

time: 98.6 us -> 144 us (1.46)
  Pallas kernels: 96.4 us -> 142 us
    pallas_call x1, Pallas kernels: 96.4 us -> 142 us  [on_device(): pl.pallas_call(functools.partial(kernel, side), out_shape=jax.ShapeDtypeS...]
where the time goes in v4:
time: 144 us
  Pallas kernels  142 us (99%)
  local copies, waits for them, and re-layouts  1.57 us (1%)
    pallas_call x1, Pallas kernels, on_device(): pl.pallas_call(functools.partial(kernel, side), out_shape=jax.ShapeDtypeS...  142 us

profile of v4, /device:TPU:6, one launch (start us, length us, event | category | flops | bytes accessed | tf_op | source)
XLA Modules:
  0.0 143.5 jit_solution(7683880052250620725)
XLA Ops:
  0.0 141.9 %shard_map.91 = bf16[256,256]{1,0:T(8,128)(2,1)} custom-call(bf16[256,256]{1,0:T(8,128)(2,1)} %bitcast.7, bf16[3,128,256]{2,1,0:T(8,128)(2,1)} %bitcast.6, bf16[256,128]{1,0:T(8,128)(2,1)} %ow_hbm.1, f32[1,4096]{1,0:T(1,128)} %bitcast.8, f32[3,3,256]{2,1,0:T(4,128)} %taps_hbm.1, f32[16,256]{1,0:T(8,128)} %res_hbm.1, f32[16,256]{1,0:T(8,128)} %rates_hbm.1, ...), custom_call_target="tpu_custom_call" | custom-call | tf_op jit(solution)/shard_map/pallas_call | solution.py:481
  141.9 1.6 %copy.11 = bf16[2,128,256]{2,1,0:T(8,128)(2,1)} copy(bf16[2,128,256]{2,1,0:T(8,128)(2,1)} %bitcast.5) | data formatting | bytes 262144

commit v5 on v2

--- a/solution.py
+++ b/solution.py
@@ -31,9 +31,9 @@
 def kernel(
     side, hid_hbm, w_hbm, ow_hbm, gain_hbm, taps_hbm, res_hbm, rates_hbm, skip_hbm, len_ref, out_ref,
     gain_ref, taps_ref, res_ref, rates_ref, skip_ref,
-    hraw, hs, pbuf, ssq, acc, ext, qbuf, ubuf, cbuf, gated, table, st_in, st0, st1, st2, parts, rs_out, rs_in,
+    hraw, hs, pbuf, ssq, acc, ext, qbuf, ubuf, cbuf, gated, table, st_in, st1, st2, parts, rs_out, rs_in,
     load_sem, ag_send, ag_recv, sib_send, sib_recv, rim_send, rim_recv,
-    st0_send, st0_recv, st1_send, st1_recv, st2_send, st2_recv, rs_send, rs_recv,
+    st1_send, st1_recv, st2_send, st2_recv, rs_send, rs_recv,
 ):
     n = side * side
     half = n // 2
@@ -53,6 +53,11 @@
     def at(yy, xx):
         return {"ctx": 2 * (side * yy + xx) + core}
 
+    place = rem(me, 2 * side)
+
+    def in_row(steps):
+        return {"ctx": me - place + rem(place + steps, 2 * side)}
+
     def chip_first(q):
         a = div(q, side)
         return side * a + rem(q - side * a + side - a, side)
@@ -89,8 +94,8 @@
     ]
 
     def slot_of(r, way, s):
-        place, slot = rings[r][:2]
-        return slot(rem(place + n - s, n) if way == RIGHT else rem(place + s, n))
+        spot, slot = rings[r][:2]
+        return slot(rem(spot + n - s, n) if way == RIGHT else rem(spot + s, n))
 
     def ag_copy(r, way, s, c, at_slot):
         part = rings[r][2](at_slot, c)
@@ -126,10 +131,9 @@
         loads.append(pltpu.make_async_copy(source, target, load_sem.at[6 + j]))
     for copy in loads:
         copy.start()
-    partners = [{"tp": rem(z + 1, n)}, {"tp": rem(z + n - 1, n)}, sibling, {"ctx": from_last(1)}]
-    for j in range(1, side):
-        partners.append(at(y, rem(x + j, side)))
-        partners.append(at(rem(y + j, side), x))
+    partners = [{"tp": rem(z + 1, n)}, {"tp": rem(z + n - 1, n)}, {"ctx": from_last(1)}]
+    partners += [in_row(j) for j in range(1, 2 * side)]
+    partners += [at(rem(y + j, side), x) for j in range(1, side)]
     barrier = pltpu.get_barrier_semaphore()
     for partner in partners:
         pl.semaphore_signal(barrier, inc=1, device_id=partner, device_id_type=MESH)
@@ -190,7 +194,6 @@
     take(slot_of(0, RIGHT, half))
     for r in (1, 2):
         sib_wait(r, RIGHT, 0)
-        sib_wait(r, RIGHT, half)
 
     def sib_step(s, carry):
         for r in (1, 2):
@@ -200,22 +203,22 @@
 
     lax.fori_loop(1, half, sib_step, 0)
 
-    deep = 4 if n % 4 == 0 else 1
-    span_k = deep * width
-
-    def product(i):
+    span_k = side * width
+    per = span_k // rows
+
+    def product(steps):
+        i = rem(y + steps, side)
         left = hs[:, pl.ds(pl.multiple_of(i * span_k, span_k), span_k)]
-        per = span_k // rows
         right = pbuf[pl.ds(i * per, per), :, : 3 * width].reshape(span_k, 3 * width)
         return jnp.dot(left, right, preferred_element_type=F32)
 
-    acc[...] = product(jnp.int32(0))
-
-    def project(i, carry):
-        acc[...] = acc[...] + product(i)
-        return carry
-
-    lax.fori_loop(1, n // deep, project, 0)
+    acc[...] = product(0)
+    for steps in range(1, side):
+        if steps != side // 2:
+            acc[...] = acc[...] + product(steps)
+    for r in (1, 2):
+        sib_wait(r, RIGHT, half)
+    acc[...] = acc[...] + product(side // 2)
     mean = jnp.sum(ssq[...], axis=1, keepdims=True) * (1.0 / features)
     scale = lax.rsqrt(mean + 1e-6)
     for s in range(samples):
@@ -225,16 +228,15 @@
 
     rates = rates_ref[...]
     decay = jnp.exp(-rates)
-    whole = jnp.exp(-rates * float(block))
     coef = res_ref[...] * jnp.sqrt(2.0 * rates / modes)
 
-    def powers(place, blocks):
+    def powers(spot, blocks, count):
         before, total = [], []
-        for i in range(side):
-            gap = jnp.maximum(place - 1 - i, 0).astype(F32)
+        for i in range(count):
+            gap = jnp.maximum(spot - 1 - i, 0).astype(F32)
             factor = jnp.exp(-rates * (gap * float(blocks * block)))
-            before.append(jnp.where(i < place, factor, 0.0))
-            total.append(jnp.exp(-rates * float(blocks * block * (side - 1 - i))))
+            before.append(jnp.where(i < spot, factor, 0.0))
+            total.append(jnp.exp(-rates * float(blocks * block * (count - 1 - i))))
         return before, total
 
     def filtered(s, j, first, count):
@@ -246,8 +248,8 @@
 
     def features_of(first, count):
         for s in range(samples):
-            place = lax.broadcasted_iota(jnp.int32, (count, 1), 0) + (me * block + first)
-            valid = jnp.where(place < len_ref[s], 1.0, 0.0)
+            position = lax.broadcasted_iota(jnp.int32, (count, 1), 0) + (me * block + first)
+            valid = jnp.where(position < len_ref[s], 1.0, 0.0)
             span = slice(first, first + count)
             pushed = filtered(s, 1, first, count) * filtered(s, 2, first, count) * valid
             ubuf[s, span, :] = pushed.astype(BF16).astype(F32)
@@ -271,9 +273,9 @@
     heads = gather_state(0, (zero,) * samples)
     late = jnp.exp(-rates * float(block - 8))
     for s in range(samples):
-        st0[core, s] = late * heads[s] + ends[s]
-    pair = remote(st0.at[core], st0.at[core], st0_send, st0_recv, sibling)
-    pair.start()
+        st1[place, s] = late * heads[s] + ends[s]
+    for j in range(1, 2 * side):
+        remote(st1.at[place], st1.at[place], st1_send.at[j], st1_recv.at[j], in_row(j)).start()
 
     def fill_table(m, carry):
         rate = rates_ref[pl.ds(m, 1), :]
@@ -294,32 +296,25 @@
 
         lax.fori_loop(0, block // 8, body, zero)
 
-    x_before, x_total = powers(x, 2)
+    x_before, x_total = powers(place, 1, 2 * side)
     lax.fori_loop(0, modes, fill_table, 0)
-    pair_in = remote(st0.at[1 - core], st0.at[1 - core], st0_send, st0_recv, sibling)
-    pair_in.wait_recv()
-    for s in range(samples):
-        st1[x, s] = whole * st0[0, s] + st0[1, s]
-    for j in range(1, side):
-        remote(st1.at[x], st1.at[x], st1_send.at[j], st1_recv.at[j], at(y, rem(x + j, side))).start()
-    y_before, _ = powers(y, 2 * side)
-    x_power = jnp.exp(-rates * (x.astype(F32) * float(2 * block)))
     convolve(0)
-    for j in range(1, side):
-        slot = st1.at[rem(x + side - j, side)]
+    for j in range(1, 2 * side):
+        slot = st1.at[rem(place + 2 * side - j, 2 * side)]
         remote(slot, slot, st1_send.at[j], st1_recv.at[j], sibling).wait_recv()
     for s in range(samples):
-        st2[y, s] = sum(x_total[i] * st1[i, s] for i in range(side))
+        st2[y, s] = sum(x_total[i] * st1[i, s] for i in range(2 * side))
     for j in range(1, side):
         remote(st2.at[y], st2.at[y], st2_send.at[j], st2_recv.at[j], at(rem(y + j, side), x)).start()
+    y_before, _ = powers(y, 2 * side, side)
+    x_power = jnp.exp(-rates * (place.astype(F32) * float(block)))
     convolve(1)
     for j in range(1, side):
         slot = st2.at[rem(y + side - j, side)]
         remote(slot, slot, st2_send.at[j], st2_recv.at[j], sibling).wait_recv()
     for s in range(samples):
         row = sum(y_before[i] * st2[i, s] for i in range(side))
-        at_chip = x_power * row + sum(x_before[i] * st1[i, s] for i in range(side))
-        st_in[s] = jnp.where(core == 0, at_chip, whole * at_chip + st0[0, s])
+        st_in[s] = x_power * row + sum(x_before[i] * st1[i, s] for i in range(2 * side))
 
     tall = 32
 
@@ -402,9 +397,9 @@
             if goes_far(way, c):
                 ag_sent(r, way, half, c)
     rim.wait_send()
-    pair.wait_send()
+    for j in range(1, 2 * side):
+        remote(st1.at[place], st1.at[place], st1_send.at[j], st1_recv.at[j], sibling).wait_send()
     for j in range(1, side):
-        remote(st1.at[x], st1.at[x], st1_send.at[j], st1_recv.at[j], sibling).wait_send()
         remote(st2.at[y], st2.at[y], st2_send.at[j], st2_recv.at[j], sibling).wait_send()
 
     def reduced(s, carry):
@@ -452,8 +447,7 @@
             pltpu.VMEM((samples * block, width), BF16),
             pltpu.VMEM((modes, block, width), F32),
             pltpu.VMEM(state, F32),
-            pltpu.VMEM((2,) + state, F32),
-            pltpu.VMEM((side,) + state, F32),
+            pltpu.VMEM((2 * side,) + state, F32),
             pltpu.VMEM((side,) + state, F32),
             pltpu.VMEM((2, samples * block, width), F32),
             pltpu.VMEM((2, half, CHUNKS, samples * block // CHUNKS, width), BF16),
@@ -465,10 +459,8 @@
             dma((2, 2, half + 1)),
             dma,
             dma,
-            dma,
-            dma,
-            dma((side,)),
-            dma((side,)),
+            dma((2 * side,)),
+            dma((2 * side,)),
             dma((side,)),
             dma((side,)),
             dma((2, half, CHUNKS)),

time: 98.6 us -> 96.5 us (0.979)
  Pallas kernels: 96.4 us -> 93.8 us
    pallas_call x1, Pallas kernels: 96.4 us -> 93.8 us  [on_device(): pl.pallas_call(functools.partial(kernel, side), out_shape=jax.ShapeDtypeS...]
where the time goes in v5:
time: 96.5 us; the launch traced here: 95.4 us
  Pallas kernels  93.8 us (97%)
  local copies, waits for them, and re-layouts  1.57 us (2%)
    pallas_call x1, Pallas kernels, on_device(): pl.pallas_call(functools.partial(kernel, side), out_shape=jax.ShapeDtypeS...  93.8 us

profile of v5, /device:TPU:6, one launch (start us, length us, event | category | flops | bytes accessed | tf_op | source)
XLA Modules:
  0.0 95.4 jit_solution(1246746383266384961)
XLA Ops:
  0.0 93.8 %shard_map.91 = bf16[256,256]{1,0:T(8,128)(2,1)} custom-call(bf16[256,256]{1,0:T(8,128)(2,1)} %bitcast.7, bf16[3,128,256]{2,1,0:T(8,128)(2,1)} %bitcast.6, bf16[256,128]{1,0:T(8,128)(2,1)} %ow_hbm.1, f32[1,4096]{1,0:T(1,128)} %bitcast.8, f32[3,3,256]{2,1,0:T(4,128)} %taps_hbm.1, f32[16,256]{1,0:T(8,128)} %res_hbm.1, f32[16,256]{1,0:T(8,128)} %rates_hbm.1, ...), custom_call_target="tpu_custom_call" | custom-call | tf_op jit(solution)/shard_map/pallas_call | solution.py:427
  93.8 1.6 %copy.11 = bf16[2,128,256]{2,1,0:T(8,128)(2,1)} copy(bf16[2,128,256]{2,1,0:T(8,128)(2,1)} %bitcast.5) | data formatting | bytes 262144

commit v6 on v5

--- a/solution.py
+++ b/solution.py
@@ -137,8 +137,7 @@
     barrier = pltpu.get_barrier_semaphore()
     for partner in partners:
         pl.semaphore_signal(barrier, inc=1, device_id=partner, device_id_type=MESH)
-    for copy in loads:
-        copy.wait()
+    loads[0].wait()
     pl.semaphore_wait(barrier, len(partners))
 
     def take(q):
@@ -155,8 +154,14 @@
 
     lanes = [(r, way) for r in range(3) for way in (RIGHT, LEFT)]
     mine = [z, me, me]
-    for c in range(CHUNKS):
-        for r, way in lanes:
+    chunks = [(r, way, c if way == RIGHT else (c + CHUNKS // 2) % CHUNKS) for c in range(CHUNKS) for r, way in lanes]
+    for r, way, c in chunks:
+        if r == 0:
+            ag_start(r, way, 1, c, mine[r])
+    for copy in loads[1:]:
+        copy.wait()
+    for r, way, c in chunks:
+        if r:
             ag_start(r, way, 1, c, mine[r])
     for r in (1, 2):
         sib_copy(r, RIGHT, 0, me).start()
@@ -165,10 +170,9 @@
 
     def ag_step(s, carry):
         slots = {(r, way): slot_of(r, way, s) for r, way in lanes}
-        for c in range(CHUNKS):
-            for r, way in lanes:
-                ag_arrived(r, way, s, c)
-                ag_start(r, way, s + 1, c, slots[r, way])
+        for r, way, c in chunks:
+            ag_arrived(r, way, s, c)
+            ag_start(r, way, s + 1, c, slots[r, way])
         for r, way in lanes[2:]:
             sib_copy(r, way, s, slots[r, way]).start()
         take(slots[0, RIGHT])
@@ -177,11 +181,10 @@
 
     lax.fori_loop(1, half - 1, ag_step, 0)
     slots = {(r, way): slot_of(r, way, half - 1) for r, way in lanes}
-    for c in range(CHUNKS):
-        for r, way in lanes:
-            ag_arrived(r, way, half - 1, c)
-            if goes_far(way, c):
-                ag_start(r, way, half, c, slots[r, way])
+    for r, way, c in chunks:
+        ag_arrived(r, way, half - 1, c)
+        if goes_far(way, c):
+            ag_start(r, way, half, c, slots[r, way])
     for r, way in lanes[2:]:
         sib_copy(r, way, half - 1, slots[r, way]).start()
     take(slots[0, RIGHT])

time: 96.5 us -> 94.3 us (0.977)
  Pallas kernels: 93.8 us -> 92.3 us
    pallas_call x1, Pallas kernels: 93.8 us -> 92.3 us  [on_device(): pl.pallas_call(functools.partial(kernel, side), out_shape=jax.ShapeDtypeS...]
where the time goes in v6:
time: 94.3 us; the launch traced here: 93.8 us
  Pallas kernels  92.3 us (98%)
  local copies, waits for them, and re-layouts  1.57 us (2%)
    pallas_call x1, Pallas kernels, on_device(): pl.pallas_call(functools.partial(kernel, side), out_shape=jax.ShapeDtypeS...  92.3 us

profile of v6, /device:TPU:6, one launch (start us, length us, event | category | flops | bytes accessed | tf_op | source)
XLA Modules:
  0.0 93.8 jit_solution(16476771272455231808)
XLA Ops:
  0.0 92.3 %shard_map.91 = bf16[256,256]{1,0:T(8,128)(2,1)} custom-call(bf16[256,256]{1,0:T(8,128)(2,1)} %bitcast.7, bf16[3,128,256]{2,1,0:T(8,128)(2,1)} %bitcast.6, bf16[256,128]{1,0:T(8,128)(2,1)} %ow_hbm.1, f32[1,4096]{1,0:T(1,128)} %bitcast.8, f32[3,3,256]{2,1,0:T(4,128)} %taps_hbm.1, f32[16,256]{1,0:T(8,128)} %res_hbm.1, f32[16,256]{1,0:T(8,128)} %rates_hbm.1, ...), custom_call_target="tpu_custom_call" | custom-call | tf_op jit(solution)/shard_map/pallas_call | solution.py:430
  92.3 1.6 %copy.11 = bf16[2,128,256]{2,1,0:T(8,128)(2,1)} copy(bf16[2,128,256]{2,1,0:T(8,128)(2,1)} %bitcast.5) | data formatting | bytes 262144

commit v7 on v6

--- a/solution.py
+++ b/solution.py
@@ -154,7 +154,7 @@
 
     lanes = [(r, way) for r in range(3) for way in (RIGHT, LEFT)]
     mine = [z, me, me]
-    chunks = [(r, way, c if way == RIGHT else (c + CHUNKS // 2) % CHUNKS) for c in range(CHUNKS) for r, way in lanes]
+    chunks = [(r, way, c if way == RIGHT else (c + CHUNKS // 2) % CHUNKS) for c in range(CHUNKS) for r, way in lanes[2:] + lanes[:2]]
     for r, way, c in chunks:
         if r == 0:
             ag_start(r, way, 1, c, mine[r])

time: 94.3 us -> 93.8 us (level)
  no operation moved by 1% of the time
where the time goes in v7:
time: 93.8 us; the launch traced here: 93.7 us
  Pallas kernels  92.1 us (98%)
  local copies, waits for them, and re-layouts  1.57 us (2%)
    pallas_call x1, Pallas kernels, on_device(): pl.pallas_call(functools.partial(kernel, side), out_shape=jax.ShapeDtypeS...  92.1 us

profile of v7, /device:TPU:6, one launch (start us, length us, event | category | flops | bytes accessed | tf_op | source)
XLA Modules:
  0.0 93.7 jit_solution(11693889468781984933)
XLA Ops:
  0.0 92.1 %shard_map.91 = bf16[256,256]{1,0:T(8,128)(2,1)} custom-call(bf16[256,256]{1,0:T(8,128)(2,1)} %bitcast.7, bf16[3,128,256]{2,1,0:T(8,128)(2,1)} %bitcast.6, bf16[256,128]{1,0:T(8,128)(2,1)} %ow_hbm.1, f32[1,4096]{1,0:T(1,128)} %bitcast.8, f32[3,3,256]{2,1,0:T(4,128)} %taps_hbm.1, f32[16,256]{1,0:T(8,128)} %res_hbm.1, f32[16,256]{1,0:T(8,128)} %rates_hbm.1, ...), custom_call_target="tpu_custom_call" | custom-call | tf_op jit(solution)/shard_map/pallas_call | solution.py:430
  92.1 1.6 %copy.11 = bf16[2,128,256]{2,1,0:T(8,128)(2,1)} copy(bf16[2,128,256]{2,1,0:T(8,128)(2,1)} %bitcast.5) | data formatting | bytes 262144
